TPU v7x, 32 devices: a whole 2x2x4 slice. The times are simulated.
32 devices in a mesh: groups: 2 (over x), cuts: 8 (over z, y), states: 2 (over core).
Axes of the slice: x: 2, y: 2, z: 4, core: 2. Of those that a mesh axis runs over, the one named last changes fastest.
Arguments:
- trial_states: bfloat16 [2, 512, 1024], P('states', ('groups', 'cuts')), parts along dimension 1, may hold values from -6 to 6
- scenario_ids: int32 [2, 512], P('states', ('groups', 'cuts')), parts along dimension 1, may hold values from 0 to 63
- dispatch: bfloat16 [1024, 1024], replicated, may hold values from -0.1875 to 0.1875
- bias: float32 [1024], replicated, may hold values from -3 to 3
- noise: float32 [128, 1024], P('groups'), parts along dimension 0, may hold values from -6 to 6
- cut_slopes: bfloat16 [32768, 1024], P(('groups', 'cuts')), parts along dimension 0, may hold values from -0.1875 to 0.1875
- cut_heights: float32 [32768], P(('groups', 'cuts')), parts along dimension 0, may hold values from -6 to 6
- active_counts: int32 [16], P(('groups', 'cuts')), parts along dimension 0, may hold values from 512 to 2048, as said below
Outputs:
- margins: bfloat16 [32768, 512], P(('groups', 'cuts'), 'states'), parts along dimension 0
There are 2 independent parts, one for each index of `groups`. A program takes and returns all parts, laid end to end along the dimension named above; an argument that names none is the same for every part. Nothing has to cross between parts.
Inputs may be any that keep to these rules, and one draw needn't show every extreme that they name: `scenario_ids`: each is the index of one row of noise. `active_counts`: some shard has all 2048 cuts active in every draw.
All inputs are finite; a program needn't handle non-finite values.
Results may differ from a plain program's by a relative error of at most 0.0029.
Values may be sent and summed in bfloat16 or wider, within the bound.
No kernel may reach another device: no remote copies, remote signals or barrier semaphores. Data moves between devices by JAX's collectives and lax.ppermute only.
A program may use at most 64 MiB of HBM per device.

v0:
```python
import jax
import jax.numpy as jnp
from jax import lax
from jax.sharding import PartitionSpec as P

NEG = -1e30


def combined_all(part, axis, combine):
    gathered = jax.tree.map(lambda a: lax.all_gather(a, axis), part)

    def take(source):
        return jax.tree.map(lambda a: lax.dynamic_index_in_dim(a, source, 0, False), gathered)

    return lax.fori_loop(
        1, lax.axis_size(axis), lambda source, state: combine(state, take(source)), take(0)
    )


def top_two(cands):
    first = jnp.max(cands, axis=0)
    ties = jnp.sum((cands == first[None, :]).astype(jnp.int32), axis=0)
    below = jnp.max(jnp.where(cands < first[None, :], cands, NEG), axis=0)
    return (first, jnp.where(ties >= 2, first, below))


def combine_pairs(left, right):
    return (
        jnp.maximum(left[0], right[0]),
        jnp.maximum(jnp.minimum(left[0], right[0]), jnp.maximum(left[1], right[1])),
    )


def roll_forward(trials, picks, dispatch, bias, noise):
    choose = (picks[:, None] == jnp.arange(noise.shape[0], dtype=jnp.int32)[None, :]).astype(
        jnp.float32
    )
    inflow = jnp.dot(
        choose, noise, precision=lax.Precision.HIGHEST, preferred_element_type=jnp.float32
    )
    flow = jnp.dot(trials, dispatch, preferred_element_type=jnp.float32) + bias[None, :] + inflow
    return jnp.maximum(flow, 0.0).astype(jnp.bfloat16)


def on_device(
    trial_states, scenario_ids, dispatch, bias, noise, cut_slopes, cut_heights, active_counts
):
    next_state = roll_forward(trial_states[0], scenario_ids[0], dispatch, bias, noise)
    product = lax.dot_general(
        cut_slopes,
        lax.all_gather(next_state, "cuts", axis=0, tiled=True),
        (((1,), (1,)), ((), ())),
        preferred_element_type=jnp.float32,
    )
    values = product + cut_heights[:, None]
    rows = jnp.arange(values.shape[0], dtype=jnp.int32)
    active = (rows < active_counts[0])[:, None]
    first, second = top_two(jnp.where(active, values, NEG))
    top1, top2 = combined_all((first, second), "cuts", combine_pairs)
    other = jnp.where(values >= top1[None, :], top2[None, :], top1[None, :])
    return jnp.where(active, values - other, 0.0).astype(jnp.bfloat16)


def solution(mesh):
    placed = (
        P("states", ("groups", "cuts"), None),
        P("states", ("groups", "cuts")),
        P(),
        P(),
        P("groups", None),
        P(("groups", "cuts"), None),
        P(("groups", "cuts")),
        P(("groups", "cuts")),
    )
    return jax.shard_map(
        on_device,
        mesh=mesh,
        in_specs=placed,
        out_specs=P(("groups", "cuts"), "states"),
        check_vma=False,
    )
```

profile of v0, /device:TPU:0, one launch (start us, length us, event | category | flops | bytes accessed | tf_op | source)
XLA Modules:
  0.0 81.8 jit_solution(16460183367613293142)
XLA Ops:
  0.0 0.0 copy-start
  0.0 0.0 copy-start.4
  0.0 0.0 copy-start.2
  0.0 0.0 copy-start.3
  0.8 0.9 %copy-done = bf16[1024,1024]{1,0:T(8,128)(2,1)S(1)} copy-done((bf16[1024,1024]{1,0:T(8,128)(2,1)S(1)}, bf16[1024,1024]{1,0:T(8,128)(2,1)}, u32[]{:S(2)}) %copy-start) | copy-done | bytes 2097176
  1.7 1.3 %convolution_add_fusion.2 = f32[32,1024]{1,0:T(8,128)S(1)} fusion(bf16[1024,1024]{1,0:T(8,128)(2,1)S(1)} %copy-done, bf16[1,32,1024]{2,1,0:T(8,128)(2,1)} %param.10, f32[1024]{0:T(1024)} %param.13), kind=kOutput, calls=%fused_computation.12 | convolution fusion | flops 67141632 | bytes 2297856 | tf_op jit(solution)/shard_map/dot_general | solution.py:41
  3.0 0.0 copy-done.2
  3.0 0.0 copy-done.3
  3.0 0.3 fusion.3
  3.3 33.0 %all_gather.13 = bf16[256,1024]{1,0:T(8,128)(2,1)S(1)} all-gather(bf16[32,1024]{1,0:T(8,128)(2,1)S(1)} %fusion.3), channel_id=1, replica_groups=mesh['groups'=2,'cuts'=8,'states'=2] {'cuts'}, dimensions={0}, use_global_device_ids=true | all-gather | bytes 589824 | tf_op jit(solution)/shard_map/all_gather | solution.py:51
  36.3 0.0 copy-done.4
  36.3 3.6 %select_reduce_fusion = (f32[256]{0:T(256)S(1)}, f32[2048,256]{0,1:T(8,128)S(1)}) fusion(pred[2048]{0:T(1024)(128)(4,1)S(1)} %iota_compare_fusion.2, f32[2048]{0:T(1024)S(1)} %copy-done.4, bf16[256,1024]{1,0:T(8,128)(2,1)S(1)} %all_gather.13, bf16[2048,1024]{1,0:T(8,128)(2,1)} %param.15), kind=kOutput, calls=%fused_computation.9 | convolution fusion | flops 1075314432 | bytes 6827008 | tf_op jit(solution)/shard_map/dot_general | solution.py:49
  39.9 0.0 copy-start.1
  39.9 0.4 fusion.1
  40.3 0.5 convert_reduce_fusion
  40.8 0.4 copy-done.1
  41.2 20.7 %all-gather.3 = f32[8,1,256]{2,1,0:T(1,128)S(1)} all-gather(f32[1,1,256]{2,1,0:T(1,128)S(1)} %bitcast.35), channel_id=3, replica_groups=mesh['groups'=2,'cuts'=8,'states'=2] {'cuts'}, dimensions={0}, use_global_device_ids=true | all-gather | bytes 9216 | tf_op jit(solution)/shard_map/all_gather | solution.py:10
  61.9 16.3 %all-gather.2 = f32[8,1,256]{2,1,0:T(1,128)S(1)} all-gather(f32[1,1,256]{2,1,0:T(1,128)S(1)} %bitcast.34), channel_id=2, replica_groups=mesh['groups'=2,'cuts'=8,'states'=2] {'cuts'}, dimensions={0}, use_global_device_ids=true | all-gather | bytes 9216 | tf_op jit(solution)/shard_map/all_gather | solution.py:10
  78.2 0.3 while.17
  78.5 2.0 %select_convert_fusion = bf16[2048,256]{0,1:T(8,128)(2,1)S(1)} fusion(f32[2048,256]{0,1:T(8,128)} %copy-done.1, f32[256]{0:T(256)S(1)} %get-tuple-element.139, f32[256]{0:T(256)S(1)} %get-tuple-element.138, pred[2048]{0:T(1024)(128)(4,1)S(1)} %iota_compare_fusion.2), kind=kLoop, calls=%fused_computation.7 | loop fusion | flops 2621440 | bytes 3149824 | tf_op jit(solution)/shard_map/convert_element_type | solution.py:61
  80.5 1.3 %copy.10 = bf16[2048,256]{1,0:T(8,128)(2,1)} copy(bf16[2048,256]{0,1:T(8,128)(2,1)S(1)} %select_convert_fusion) | data formatting | bytes 2097152 | tf_op jit(solution)/shard_map/convert_element_type | solution.py:61
  (20 shorter events, 0.2 us)
Async XLA Ops:
  0.0 1.7 %copy-start = (bf16[1024,1024]{1,0:T(8,128)(2,1)S(1)}, bf16[1024,1024]{1,0:T(8,128)(2,1)}, u32[]{:S(2)}) copy-start(bf16[1024,1024]{1,0:T(8,128)(2,1)} %param.12) | copy-start | bytes 6291460
  0.0 36.3 %copy-start.4 = (f32[2048]{0:T(1024)S(1)}, f32[2048]{0:T(1024)}, u32[]{:S(2)}) copy-start(f32[2048]{0:T(1024)} %param.16) | copy-start | bytes 24580
  0.0 3.0 %copy-start.2 = (f32[64,1024]{1,0:T(8,128)S(1)}, f32[64,1024]{1,0:T(8,128)}, u32[]{:S(2)}) copy-start(f32[64,1024]{1,0:T(8,128)} %param.14) | copy-start | bytes 786436
  0.0 3.0 %copy-start.3 = (s32[1,32]{1,0:T(1,128)S(1)}, s32[1,32]{1,0:T(1,128)}, u32[]{:S(2)}) copy-start(s32[1,32]{1,0:T(1,128)} %param.11) | copy-start | bytes 388
  39.9 1.4 %copy-start.1 = (f32[2048,256]{0,1:T(8,128)}, f32[2048,256]{0,1:T(8,128)S(1)}, u32[]{:S(2)}) copy-start(f32[2048,256]{0,1:T(8,128)S(1)} %get-tuple-element.155) | copy-start | bytes 6291460
where the time goes:
time: 82.1 us; the launch traced here: 81.8 us
  blocking collectives  69.9 us (85%)
  matrix products  5.13 us (6%)
  other arithmetic  3.03 us (4%)
  local copies, waits for them, and re-layouts  2.68 us (3%)
  between operations  0.87 us (1%)
    all_gather x2, blocking collectives, combined_all(): gathered = jax.tree.map(lambda a: lax.all_gather(a, axis), part)  36.9 us
    all_gather x1, blocking collectives, on_device(): lax.all_gather(next_state, 'cuts', axis=0, tiled=True)  33 us
    dot_general x1, matrix products, on_device(): lax.dot_general(cut_slopes, lax.all_gather(next_state, 'cuts', axis=0, ti...  3.57 us
    convert_element_type x1, other arithmetic, on_device(): return jnp.where(active, values - other, 0.0).astype(jnp.bfloat16)  2 us

commit v1 on v0

v1 whole, which is shorter than its diff:
```python
import functools

import jax
import jax.numpy as jnp
from jax import lax
from jax.experimental import pallas as pl
from jax.experimental.pallas import tpu as pltpu
from jax.sharding import PartitionSpec as P

NEG = -1e30
MIB = 1024 * 1024
LANES = 128
LAST = (3, 2, 1)
VMEM = pl.BlockSpec(memory_space=pltpu.VMEM)
HBM = pl.BlockSpec(memory_space=pltpu.HBM)
SMEM = pl.BlockSpec(memory_space=pltpu.SMEM)


def swap(array, step):
    n = lax.axis_size("cuts")
    return lax.ppermute(array, "cuts", [(i, i ^ step) for i in range(n)])


def early_steps(n):
    steps, step = [], n // 2
    while step >= 4:
        steps.append(step)
        step //= 2
    return steps


def merge(left, right):
    high, low = jnp.maximum(left[0:1], right[0:1]), jnp.minimum(left[0:1], right[0:1])
    return jnp.concatenate([high, jnp.maximum(low, jnp.maximum(left[1:2], right[1:2]))], axis=0)


def split_in_three(values):
    high = values.astype(jnp.bfloat16)
    rest = values - high.astype(jnp.float32)
    mid = rest.astype(jnp.bfloat16)
    return high, mid, (rest - mid.astype(jnp.float32)).astype(jnp.bfloat16)


def roll(trials, ids, dispatch_ref, bias, noise_ref):
    scenarios = lax.broadcasted_iota(jnp.int32, (noise_ref.shape[0] // 3, ids.shape[1]), 0)
    chosen = jnp.where(scenarios == ids, 1.0, 0.0)
    chosen = jnp.concatenate([chosen] * 3, axis=0).astype(jnp.bfloat16)
    inflow = lax.dot_general(
        chosen, noise_ref[...], (((0,), (0,)), ((), ())), preferred_element_type=jnp.float32
    )
    flow = jnp.dot(trials, dispatch_ref[...], preferred_element_type=jnp.float32)
    return jnp.maximum(flow + bias + inflow, 0.0).astype(jnp.bfloat16)


def stage_kernel(
    trials_hbm, ids_hbm, dispatch_hbm, bias_hbm, noise_hbm, heights_hbm, slopes_hbm,
    own_ref, dispatch_ref, bias_ref, noise3_ref, columns_ref, slopes_ref,
    trials_ref, ids_ref, noise_ref, heights_ref, sems,
):
    pairs = (
        (noise_hbm, noise_ref),
        (trials_hbm, trials_ref),
        (ids_hbm, ids_ref),
        (bias_hbm, bias_ref),
        (heights_hbm, heights_ref),
        (dispatch_hbm, dispatch_ref),
        (slopes_hbm, slopes_ref),
    )
    copies = [pltpu.make_async_copy(src, dst, sems.at[i]) for i, (src, dst) in enumerate(pairs)]
    for copy in copies:
        copy.start()
    copies[0].wait()
    scenarios = noise_ref.shape[0]
    for i, term in enumerate(split_in_three(noise_ref[...])):
        noise3_ref[i * scenarios : (i + 1) * scenarios, :] = term
    for copy in copies[1:5]:
        copy.wait()
    for i in range(heights_ref.shape[0]):
        column = jnp.broadcast_to(heights_ref[i : i + 1, :], (LANES, LANES)).T
        columns_ref[i * LANES : (i + 1) * LANES, :] = column
    copies[5].wait()
    own_ref[...] = roll(trials_ref[...], ids_ref[...], dispatch_ref, bias_ref[...], noise3_ref)
    copies[6].wait()


def roll_kernel(own_ref, other_ref, ids_ref, dispatch_ref, bias_ref, noise3_ref, out_ref):
    rows = own_ref.shape[0]
    out_ref[0:rows, :] = own_ref[...]
    out_ref[rows:, :] = roll(other_ref[...], ids_ref[...], dispatch_ref, bias_ref[...], noise3_ref)


def sublane_top_two(first, second):
    size = first.shape[0]
    while size > 1:
        half = size // 2
        a1, b1, a2, b2 = first[:half], first[half:size], second[:half], second[half:size]
        first, second = jnp.maximum(a1, b1), jnp.maximum(jnp.minimum(a1, b1), jnp.maximum(a2, b2))
        size = half
    return first, second


def values_kernel(offsets, block, *refs):
    counts_ref, slopes_ref, heights_ref = refs[:3]
    pieces, (values_ref, tops_ref, states_ref) = refs[3:-3], refs[-3:]
    me = lax.axis_index("cuts")
    held = len(offsets) // len(pieces)
    rows = pieces[0].shape[0] // held
    for i, offset in enumerate(offsets):
        piece, slot = pieces[i // held], i % held
        start = pl.multiple_of((me ^ offset) * rows, rows)
        states_ref[pl.ds(start, rows), :] = piece[slot * rows : (slot + 1) * rows, :]
    count = counts_ref[0]
    cuts, chunk = slopes_ref.shape[0], min(512, slopes_ref.shape[0])

    def on_block(column):
        states = states_ref[pl.ds(column, block), :]
        first = jnp.full((8, block), NEG, jnp.float32)
        second = first
        for start in range(0, cuts, chunk):
            here = lax.dot_general(
                slopes_ref[start : start + chunk, :],
                states,
                (((1,), (1,)), ((), ())),
                preferred_element_type=jnp.float32,
            )
            heights = heights_ref[start : start + chunk, :]
            here = here + jnp.concatenate([heights] * (block // LANES), axis=1)
            values_ref[start : start + chunk, pl.ds(column, block)] = here
            row = lax.broadcasted_iota(jnp.int32, (chunk, block), 0) + start
            here = jnp.where(row < count, here, NEG)
            for sub in range(0, chunk, 8):
                v = here[sub : sub + 8]
                second = jnp.maximum(second, jnp.minimum(first, v))
                first = jnp.maximum(first, v)
        first, second = sublane_top_two(first, second)
        tops_ref[0:1, pl.ds(column, block)] = first
        tops_ref[1:2, pl.ds(column, block)] = second

    blocks = states_ref.shape[0] // block
    if blocks == 1:
        on_block(0)
    else:

        @pl.loop(0, blocks)
        def _(b):
            on_block(pl.multiple_of(b * block, block))


def margins_kernel(chunk, counts_ref, values_ref, *refs):
    tops, (out_ref, held_ref, sems) = refs[:-3], refs[-3:]
    total = tops[0][...]
    for other in tops[1:]:
        total = merge(total, other[...])
    top1, top2 = total[0:1], total[1:2]
    count = counts_ref[0]
    cuts = values_ref.shape[0]
    copies = []
    for i in range(cuts // chunk):
        rows = slice(i * chunk, (i + 1) * chunk)
        values = values_ref[rows, :]
        row = lax.broadcasted_iota(jnp.int32, values.shape, 0) + i * chunk
        margin = values - jnp.where(values >= top1, top2, top1)
        held_ref[rows, :] = jnp.where(row < count, margin, 0.0).astype(jnp.bfloat16)
        copy = pltpu.make_async_copy(held_ref.at[rows], out_ref.at[rows], sems.at[i])
        copy.start()
        copies.append(copy)
    for copy in copies:
        copy.wait()


def on_device(
    trial_states, scenario_ids, dispatch, bias, noise, cut_slopes, cut_heights, active_counts
):
    n = lax.axis_size("cuts")
    steps = early_steps(n)
    trials = trial_states[0]
    rows, width = trials.shape
    half, cuts = rows * n, cut_slopes.shape[0]

    other, other_ids = swap(trials, steps[0]), swap(scenario_ids, steps[0])
    scenarios = noise.shape[0]
    heights = cut_heights.reshape(cuts // LANES, LANES)
    sources = (trials, scenario_ids, dispatch, bias[None, :], noise, heights, cut_slopes)
    own, dispatch, bias, noise3, heights, slopes = pl.pallas_call(
        stage_kernel,
        out_shape=(
            jax.ShapeDtypeStruct((rows, width), jnp.bfloat16),
            jax.ShapeDtypeStruct(dispatch.shape, dispatch.dtype),
            jax.ShapeDtypeStruct((1, width), jnp.float32),
            jax.ShapeDtypeStruct((3 * scenarios, width), jnp.bfloat16),
            jax.ShapeDtypeStruct((cuts, LANES), jnp.float32),
            jax.ShapeDtypeStruct(cut_slopes.shape, cut_slopes.dtype),
        ),
        in_specs=[HBM] * 7,
        out_specs=(VMEM,) * 6,
        scratch_shapes=[
            pltpu.VMEM((rows, width), jnp.bfloat16),
            pltpu.VMEM(scenario_ids.shape, jnp.int32),
            pltpu.VMEM(noise.shape, jnp.float32),
            pltpu.VMEM((cuts // LANES, LANES), jnp.float32),
            pltpu.SemaphoreType.DMA((7,)),
        ],
        compiler_params=pltpu.CompilerParams(vmem_limit_bytes=16 * MIB),
        cost_estimate=pl.CostEstimate(
            flops=2 * rows * width * width,
            bytes_accessed=2 * width * (width + cuts),
            transcendentals=0,
        ),
        name="stage",
    )(*(pltpu.with_memory_space_constraint(array, pltpu.HBM) for array in sources))
    held = pl.pallas_call(
        roll_kernel,
        out_shape=jax.ShapeDtypeStruct((2 * rows, width), jnp.bfloat16),
        in_specs=[VMEM] * 6,
        out_specs=VMEM,
        compiler_params=pltpu.CompilerParams(vmem_limit_bytes=16 * MIB),
        cost_estimate=pl.CostEstimate(
            flops=2 * rows * width * width, bytes_accessed=2 * width * width, transcendentals=0
        ),
        name="roll_forward",
    )(own, other, other_ids, dispatch, bias, noise3)
    offsets = [0, steps[0]]
    for step in steps[1:]:
        held = jnp.concatenate([held, swap(held, step)], axis=0)
        offsets = offsets + [offset ^ step for offset in offsets]
    pieces = [held] + [swap(held, step) for step in LAST]
    offsets = [offset ^ step for step in (0, *LAST) for offset in offsets]

    values, tops = pl.pallas_call(
        functools.partial(values_kernel, offsets, min(256, half)),
        out_shape=(
            jax.ShapeDtypeStruct((cuts, half), jnp.float32),
            jax.ShapeDtypeStruct((2, half), jnp.float32),
        ),
        in_specs=[SMEM] + [VMEM] * (2 + len(pieces)),
        out_specs=(VMEM, VMEM),
        scratch_shapes=[pltpu.VMEM((half, width), jnp.bfloat16)],
        compiler_params=pltpu.CompilerParams(vmem_limit_bytes=32 * MIB),
        cost_estimate=pl.CostEstimate(
            flops=2 * cuts * half * width, bytes_accessed=2 * cuts * width, transcendentals=0
        ),
        name="cut_values",
    )(active_counts, slopes, heights, *pieces)

    for step in steps:
        tops = merge(tops, swap(tops, step))
    sets = [tops] + [swap(tops, step) for step in LAST]

    chunk = min(256, cuts)
    return pl.pallas_call(
        functools.partial(margins_kernel, chunk),
        out_shape=jax.ShapeDtypeStruct((cuts, half), jnp.bfloat16),
        in_specs=[SMEM] + [VMEM] * (1 + len(sets)),
        out_specs=pl.BlockSpec(memory_space=pl.ANY),
        scratch_shapes=[
            pltpu.VMEM((cuts, half), jnp.bfloat16),
            pltpu.SemaphoreType.DMA((cuts // chunk,)),
        ],
        compiler_params=pltpu.CompilerParams(vmem_limit_bytes=16 * MIB),
        cost_estimate=pl.CostEstimate(
            flops=4 * cuts * half, bytes_accessed=2 * cuts * half, transcendentals=0
        ),
        name="margins",
    )(active_counts, values, *sets)


def solution(mesh):
    placed = (
        P("states", ("groups", "cuts"), None),
        P("states", ("groups", "cuts")),
        P(),
        P(),
        P("groups", None),
        P(("groups", "cuts"), None),
        P(("groups", "cuts")),
        P(("groups", "cuts")),
    )
    return jax.shard_map(
        on_device,
        mesh=mesh,
        in_specs=placed,
        out_specs=P(("groups", "cuts"), "states"),
        check_vma=False,
    )
```

time: 82.1 us -> 31.6 us (0.38)
  blocking collectives: 69.9 us -> 0 us
  starting transfers between devices: 0 us -> 13 us
  waiting for transfers between devices: 0 us -> 11.5 us
  Pallas kernels: 0 us -> 6.2 us
  matrix products: 5.13 us -> 0 us
  other arithmetic: 3.03 us -> 0.02 us
  local copies, waits for them, and re-layouts: 2.68 us -> 0 us
    all_gather x3 -> x0, blocking collectives: 69.9 us -> none  [the longest x2 36.9 us: combined_all(): gathered = jax.tree.map(lambda a: lax.all_gather(a, axis), part)]
    ppermute x0 -> x9, starting transfers between devices: none -> 13 us  [swap(): return lax.ppermute(array, 'cuts', [(i, i ^ step) for i in range(n)])]
    ppermute x0 -> x9, waiting for transfers between devices: none -> 11.5 us  [swap(): return lax.ppermute(array, 'cuts', [(i, i ^ step) for i in range(n)])]
    pallas_call x0 -> x4, Pallas kernels: none -> 6.2 us  [the longest x1 3.06 us: on_device(): pl.pallas_call(stage_kernel, out_shape=(jax.ShapeDtypeStruct((rows, width...]
    dot_general x3 -> x0, matrix products: 5.13 us -> none  [the longest x1 3.57 us: on_device(): lax.dot_general(cut_slopes, lax.all_gather(next_state, 'cuts', axis=0, ti...]
    convert_element_type x1 -> x0, other arithmetic: 2 us -> none  [on_device(): return jnp.where(active, values - other, 0.0).astype(jnp.bfloat16)]
    unnamed x12 -> x0, local copies, waits for them, and re-layouts: 1.31 us -> none
    convert_element_type x1 -> x0, local copies, waits for them, and re-layouts: 1.31 us -> none  [on_device(): return jnp.where(active, values - other, 0.0).astype(jnp.bfloat16)]
  transfers between devices with their start and end apart: 0 -> 9, of which waited for: 0 -> 8; matrix products, arithmetic and copies ran while one was open for 0% -> 0% of each run, Pallas kernels for 0% -> 10%
where the time goes in v1:
time: 31.6 us; the launch traced here: 31.4 us
  starting transfers between devices  13 us (41%)
  waiting for transfers between devices  11.5 us (36%)
  Pallas kernels  6.2 us (20%)
  between operations  0.68 us (2%)
    ppermute x9, starting transfers between devices, swap(): return lax.ppermute(array, 'cuts', [(i, i ^ step) for i in range(n)])  13 us
    ppermute x9, waiting for transfers between devices, swap(): return lax.ppermute(array, 'cuts', [(i, i ^ step) for i in range(n)])  11.5 us
    pallas_call x1, Pallas kernels, on_device(): pl.pallas_call(stage_kernel, out_shape=(jax.ShapeDtypeStruct((rows, width...  3.06 us
    pallas_call x1, Pallas kernels, on_device(): pl.pallas_call(functools.partial(values_kernel, offsets, min(256, half)),...  1.46 us
    pallas_call x1, Pallas kernels, on_device(): pl.pallas_call(functools.partial(margins_kernel, chunk), out_shape=jax.Sh...  1.11 us
  transfers between devices with their start and end apart: 9, of which 8 were waited for; matrix products, arithmetic and copies ran while one was open for 0% of the time, Pallas kernels for 10%

profile of v1, /device:TPU:0, one launch (start us, length us, event | category | flops | bytes accessed | tf_op | source)
XLA Modules:
  0.0 31.4 jit_solution(2167256379441779703)
XLA Ops:
  0.0 4.0 %collective-permute-start = (bf16[32,1024]{1,0:T(8,128)(2,1)}, bf16[32,1024]{1,0:T(8,128)(2,1)S(1)}, u32[]{:S(2)}, u32[]{:S(2)}) collective-permute-start(bf16[32,1024]{1,0:T(8,128)(2,1)} %bitcast.3), channel_id=1, source_target_pairs={{0,8},{2,10},{4,12},{6,14},{8,0},{10,2},{12,4},{14,6},{1,9},{3,11}... | collective-permute-start | bytes 196616 | tf_op jit(solution)/shard_map/ppermute | solution.py:21
  4.0 0.0 collective-permute-start.1
  4.1 3.1 %stage.1 = (bf16[32,1024]{1,0:T(8,128)(2,1)S(1)}, bf16[1024,1024]{1,0:T(8,128)(2,1)S(1)}, f32[1,1024]{1,0:T(1,128)S(1)}, bf16[192,1024]{1,0:T(8,128)(2,1)S(1)}, ...) custom-call(bf16[32,1024]{1,0:T(8,128)(2,1)} %bitcast.4, s32[1,32]{1,0:T(1,128)} %ids_hbm.1, ...), custom_call_target="tpu_custom_call" | custom-call | flops 67108864 | bytes 6291456 | tf_op jit(solution)/shard_map/stage/pallas_call | solution.py:184
  7.1 1.5 %collective-permute-done.1.ids_ref = s32[1,32]{1,0:T(1,128)S(1)} collective-permute-done((s32[1,32]{1,0:T(1,128)}, s32[1,32]{1,0:T(1,128)S(1)}, u32[]{:S(2)}, u32[]{:S(2)}) %collective-permute-start.1) | collective-permute-done | bytes 160 | tf_op jit(solution)/shard_map/ppermute | solution.py:21
  8.6 0.0 collective-permute-done.other_ref
  8.6 0.6 %roll_forward.1.refs_3_ = bf16[64,1024]{1,0:T(8,128)(2,1)S(1)} custom-call(bf16[32,1024]{1,0:T(8,128)(2,1)S(1)} %get-tuple-element.15.own_ref, bf16[32,1024]{1,0:T(8,128)(2,1)S(1)} %collective-permute-done.other_ref, s32[1,32]{1,0:T(1,128)S(1)} %collective-permute-done.1.ids_ref, bf16[1024,1024]{1,0:T(8,128)(2,1)S(1)} %get-tuple-element.16.dispatch_ref, ...), custom_call_target="tpu_custom_call" | custom-call | flops 67108864 | bytes 2097152 | tf_op jit(solution)/shard_map/roll_forward/pallas_call | solution.py:211
  9.2 2.6 %collective-permute-start.2 = (bf16[64,1024]{1,0:T(8,128)(2,1)S(1)}, bf16[64,1024]{1,0:T(8,128)(2,1)S(1)}, u32[]{:S(2)}, u32[]{:S(2)}) collective-permute-start(bf16[64,1024]{1,0:T(8,128)(2,1)S(1)} %roll_forward.1.refs_3_), channel_id=1, source_target_pairs={{0,6},{2,4},{4,2},{6,0},{8,14},{10,12},{12,10},{14,8},{1,7},{3,5},... | collective-permute-start | bytes 393224 | tf_op jit(solution)/shard_map/ppermute | solution.py:21
  11.7 0.4 %collective-permute-start.3 = (bf16[64,1024]{1,0:T(8,128)(2,1)S(1)}, bf16[64,1024]{1,0:T(8,128)(2,1)S(1)}, u32[]{:S(2)}, u32[]{:S(2)}) collective-permute-start(bf16[64,1024]{1,0:T(8,128)(2,1)S(1)} %roll_forward.1.refs_3_), channel_id=1, source_target_pairs={{0,4},{2,6},{4,0},{6,2},{8,12},{10,14},{12,8},{14,10},{1,5},{3,7},... | collective-permute-start | bytes 393224 | tf_op jit(solution)/shard_map/ppermute | solution.py:21
  12.2 0.5 %collective-permute-start.4 = (bf16[64,1024]{1,0:T(8,128)(2,1)S(1)}, bf16[64,1024]{1,0:T(8,128)(2,1)S(1)}, u32[]{:S(2)}, u32[]{:S(2)}) collective-permute-start(bf16[64,1024]{1,0:T(8,128)(2,1)S(1)} %roll_forward.1.refs_3_), channel_id=1, source_target_pairs={{0,2},{2,0},{4,6},{6,4},{8,10},{10,8},{12,14},{14,12},{1,3},{3,1},... | collective-permute-start | bytes 393224 | tf_op jit(solution)/shard_map/ppermute | solution.py:21
  13.3 3.0 %collective-permute-done.2.refs_4_ = bf16[64,1024]{1,0:T(8,128)(2,1)S(1)} collective-permute-done((bf16[64,1024]{1,0:T(8,128)(2,1)S(1)}, bf16[64,1024]{1,0:T(8,128)(2,1)S(1)}, u32[]{:S(2)}, u32[]{:S(2)}) %collective-permute-start.2) | collective-permute-done | bytes 131104 | tf_op jit(solution)/shard_map/ppermute | solution.py:21
  16.4 1.3 %collective-permute-done.3.refs_5_ = bf16[64,1024]{1,0:T(8,128)(2,1)S(1)} collective-permute-done((bf16[64,1024]{1,0:T(8,128)(2,1)S(1)}, bf16[64,1024]{1,0:T(8,128)(2,1)S(1)}, u32[]{:S(2)}, u32[]{:S(2)}) %collective-permute-start.3) | collective-permute-done | bytes 131104 | tf_op jit(solution)/shard_map/ppermute | solution.py:21
  17.7 0.1 collective-permute-done.4.refs_6_
  17.8 1.5 %cut_values.1 = (f32[2048,256]{1,0:T(8,128)S(1)}, f32[2,256]{1,0:T(2,128)S(1)}) custom-call(s32[1]{0:T(128)S(6)} %copy.9.refs_0_.counts_ref, bf16[2048,1024]{1,0:T(8,128)(2,1)S(1)} %get-tuple-element.13.refs_1_, f32[2048,128]{1,0:T(8,128)S(1)} %get-tuple-element.14.refs_2_, bf16[64,1024]{1,0:T(8,128)(2,1)S(1)} %roll_forward.1.refs_3_, ...), custom_call_target="tpu_custom_call" | custom-call | flops 1073741824 | bytes 4194304 | tf_op jit(solution)/shard_map/cut_values/pallas_call | solution.py:229
  19.2 1.9 %collective-permute-start.5 = (f32[2,256]{1,0:T(2,128)S(1)}, f32[2,256]{1,0:T(2,128)S(1)}, u32[]{:S(2)}, u32[]{:S(2)}) collective-permute-start(f32[2,256]{1,0:T(2,128)S(1)} %get-tuple-element.20), channel_id=1, source_target_pairs={{0,8},{2,10},{4,12},{6,14},{8,0},{10,2},{12,4},{14,6},{1,9},{3,11}... | collective-permute-start | bytes 6152 | tf_op jit(solution)/shard_map/ppermute | solution.py:21
  21.1 2.7 %collective-permute-done.5 = f32[2,256]{1,0:T(2,128)S(1)} collective-permute-done((f32[2,256]{1,0:T(2,128)S(1)}, f32[2,256]{1,0:T(2,128)S(1)}, u32[]{:S(2)}, u32[]{:S(2)}) %collective-permute-start.5) | collective-permute-done | bytes 2080 | tf_op jit(solution)/shard_map/ppermute | solution.py:21
  23.8 1.6 %collective-permute-start.6 = (f32[2,256]{1,0:T(2,128)S(1)}, f32[2,256]{1,0:T(2,128)S(1)}, u32[]{:S(2)}, u32[]{:S(2)}) collective-permute-start(f32[2,256]{1,0:T(2,128)S(1)} %pad_maximum_fusion.refs_0_), channel_id=1, source_target_pairs={{0,6},{2,4},{4,2},{6,0},{8,14},{10,12},{12,10},{14,8},{1,7},{3,5},... | collective-permute-start | bytes 6152 | tf_op jit(solution)/shard_map/ppermute | solution.py:21
  25.4 1.4 %collective-permute-start.7 = (f32[2,256]{1,0:T(2,128)S(1)}, f32[2,256]{1,0:T(2,128)S(1)}, u32[]{:S(2)}, u32[]{:S(2)}) collective-permute-start(f32[2,256]{1,0:T(2,128)S(1)} %pad_maximum_fusion.refs_0_), channel_id=1, source_target_pairs={{0,4},{2,6},{4,0},{6,2},{8,12},{10,14},{12,8},{14,10},{1,5},{3,7},... | collective-permute-start | bytes 6152 | tf_op jit(solution)/shard_map/ppermute | solution.py:21
  26.7 0.6 %collective-permute-start.8 = (f32[2,256]{1,0:T(2,128)S(1)}, f32[2,256]{1,0:T(2,128)S(1)}, u32[]{:S(2)}, u32[]{:S(2)}) collective-permute-start(f32[2,256]{1,0:T(2,128)S(1)} %pad_maximum_fusion.refs_0_), channel_id=1, source_target_pairs={{0,2},{2,0},{4,6},{6,4},{8,10},{10,8},{12,14},{14,12},{1,3},{3,1},... | collective-permute-start | bytes 6152 | tf_op jit(solution)/shard_map/ppermute | solution.py:21
  27.4 1.0 %collective-permute-done.6.refs_1_ = f32[2,256]{1,0:T(2,128)S(1)} collective-permute-done((f32[2,256]{1,0:T(2,128)S(1)}, f32[2,256]{1,0:T(2,128)S(1)}, u32[]{:S(2)}, u32[]{:S(2)}) %collective-permute-start.6) | collective-permute-done | bytes 2080 | tf_op jit(solution)/shard_map/ppermute | solution.py:21
  28.3 0.6 %collective-permute-done.7.refs_2_ = f32[2,256]{1,0:T(2,128)S(1)} collective-permute-done((f32[2,256]{1,0:T(2,128)S(1)}, f32[2,256]{1,0:T(2,128)S(1)}, u32[]{:S(2)}, u32[]{:S(2)}) %collective-permute-start.7) | collective-permute-done | bytes 2080 | tf_op jit(solution)/shard_map/ppermute | solution.py:21
  29.0 1.4 %collective-permute-done.8.refs_3_ = f32[2,256]{1,0:T(2,128)S(1)} collective-permute-done((f32[2,256]{1,0:T(2,128)S(1)}, f32[2,256]{1,0:T(2,128)S(1)}, u32[]{:S(2)}, u32[]{:S(2)}) %collective-permute-start.8) | collective-permute-done | bytes 2080 | tf_op jit(solution)/shard_map/ppermute | solution.py:21
  30.3 1.1 %margins.1 = bf16[2048,256]{1,0:T(8,128)(2,1)} custom-call(s32[1]{0:T(128)S(6)} %copy.9.refs_0_.counts_ref, f32[2048,256]{1,0:T(8,128)S(1)} %get-tuple-element.19.values_ref, f32[2,256]{1,0:T(2,128)S(1)} %pad_maximum_fusion.refs_0_, f32[2,256]{1,0:T(2,128)S(1)} %collective-permute-done.6.refs_1_, f32[2,256]{1,0:T(2,128)S(1)} %collective-permute-done.7.refs_2_, ...), custom_call_target="tpu_custom_call" | custom-call | flops 2097152 | bytes 1048576 | tf_op jit(solution)/shard_map/margins/pallas_call | solution.py:250
  (2 shorter events, 0.0 us)
Async XLA Ops:
  0.0 8.6 %collective-permute-start = (bf16[32,1024]{1,0:T(8,128)(2,1)}, bf16[32,1024]{1,0:T(8,128)(2,1)S(1)}, u32[]{:S(2)}, u32[]{:S(2)}) collective-permute-start(bf16[32,1024]{1,0:T(8,128)(2,1)} %bitcast.3), channel_id=1, source_target_pairs={{0,8},{2,10},{4,12},{6,14},{8,0},{10,2},{12,4},{14,6},{1,9},{3,11}... | collective-permute-start | bytes 196616 | tf_op jit(solution)/shard_map/ppermute | solution.py:21
  4.0 4.6 %collective-permute-start.1 = (s32[1,32]{1,0:T(1,128)}, s32[1,32]{1,0:T(1,128)S(1)}, u32[]{:S(2)}, u32[]{:S(2)}) collective-permute-start(s32[1,32]{1,0:T(1,128)} %ids_hbm.1), channel_id=1, source_target_pairs={{0,8},{2,10},{4,12},{6,14},{8,0},{10,2},{12,4},{14,6},{1,9},{3,11}... | collective-permute-start | bytes 392 | tf_op jit(solution)/shard_map/ppermute | solution.py:21
  9.2 7.2 %collective-permute-start.2 = (bf16[64,1024]{1,0:T(8,128)(2,1)S(1)}, bf16[64,1024]{1,0:T(8,128)(2,1)S(1)}, u32[]{:S(2)}, u32[]{:S(2)}) collective-permute-start(bf16[64,1024]{1,0:T(8,128)(2,1)S(1)} %roll_forward.1.refs_3_), channel_id=1, source_target_pairs={{0,6},{2,4},{4,2},{6,0},{8,14},{10,12},{12,10},{14,8},{1,7},{3,5},... | collective-permute-start | bytes 393224 | tf_op jit(solution)/shard_map/ppermute | solution.py:21
  11.7 6.0 %collective-permute-start.3 = (bf16[64,1024]{1,0:T(8,128)(2,1)S(1)}, bf16[64,1024]{1,0:T(8,128)(2,1)S(1)}, u32[]{:S(2)}, u32[]{:S(2)}) collective-permute-start(bf16[64,1024]{1,0:T(8,128)(2,1)S(1)} %roll_forward.1.refs_3_), channel_id=1, source_target_pairs={{0,4},{2,6},{4,0},{6,2},{8,12},{10,14},{12,8},{14,10},{1,5},{3,7},... | collective-permute-start | bytes 393224 | tf_op jit(solution)/shard_map/ppermute | solution.py:21
  12.2 5.6 %collective-permute-start.4 = (bf16[64,1024]{1,0:T(8,128)(2,1)S(1)}, bf16[64,1024]{1,0:T(8,128)(2,1)S(1)}, u32[]{:S(2)}, u32[]{:S(2)}) collective-permute-start(bf16[64,1024]{1,0:T(8,128)(2,1)S(1)} %roll_forward.1.refs_3_), channel_id=1, source_target_pairs={{0,2},{2,0},{4,6},{6,4},{8,10},{10,8},{12,14},{14,12},{1,3},{3,1},... | collective-permute-start | bytes 393224 | tf_op jit(solution)/shard_map/ppermute | solution.py:21
  19.2 4.5 %collective-permute-start.5 = (f32[2,256]{1,0:T(2,128)S(1)}, f32[2,256]{1,0:T(2,128)S(1)}, u32[]{:S(2)}, u32[]{:S(2)}) collective-permute-start(f32[2,256]{1,0:T(2,128)S(1)} %get-tuple-element.20), channel_id=1, source_target_pairs={{0,8},{2,10},{4,12},{6,14},{8,0},{10,2},{12,4},{14,6},{1,9},{3,11}... | collective-permute-start | bytes 6152 | tf_op jit(solution)/shard_map/ppermute | solution.py:21
  23.8 4.5 %collective-permute-start.6 = (f32[2,256]{1,0:T(2,128)S(1)}, f32[2,256]{1,0:T(2,128)S(1)}, u32[]{:S(2)}, u32[]{:S(2)}) collective-permute-start(f32[2,256]{1,0:T(2,128)S(1)} %pad_maximum_fusion.refs_0_), channel_id=1, source_target_pairs={{0,6},{2,4},{4,2},{6,0},{8,14},{10,12},{12,10},{14,8},{1,7},{3,5},... | collective-permute-start | bytes 6152 | tf_op jit(solution)/shard_map/ppermute | solution.py:21
  25.4 3.6 %collective-permute-start.7 = (f32[2,256]{1,0:T(2,128)S(1)}, f32[2,256]{1,0:T(2,128)S(1)}, u32[]{:S(2)}, u32[]{:S(2)}) collective-permute-start(f32[2,256]{1,0:T(2,128)S(1)} %pad_maximum_fusion.refs_0_), channel_id=1, source_target_pairs={{0,4},{2,6},{4,0},{6,2},{8,12},{10,14},{12,8},{14,10},{1,5},{3,7},... | collective-permute-start | bytes 6152 | tf_op jit(solution)/shard_map/ppermute | solution.py:21
  26.7 3.6 %collective-permute-start.8 = (f32[2,256]{1,0:T(2,128)S(1)}, f32[2,256]{1,0:T(2,128)S(1)}, u32[]{:S(2)}, u32[]{:S(2)}) collective-permute-start(f32[2,256]{1,0:T(2,128)S(1)} %pad_maximum_fusion.refs_0_), channel_id=1, source_target_pairs={{0,2},{2,0},{4,6},{6,4},{8,10},{10,8},{12,14},{14,12},{1,3},{3,1},... | collective-permute-start | bytes 6152 | tf_op jit(solution)/shard_map/ppermute | solution.py:21

commit v2 on v1

--- a/solution.py
+++ b/solution.py
@@ -10,7 +10,8 @@
 NEG = -1e30
 MIB = 1024 * 1024
 LANES = 128
-LAST = (3, 2, 1)
+NEAR_STATES = (3, 1, 2)
+EARLY_TOPS, LATE_TOPS = ((1, 1), (0, 1)), (3, 2)
 VMEM = pl.BlockSpec(memory_space=pltpu.VMEM)
 HBM = pl.BlockSpec(memory_space=pltpu.HBM)
 SMEM = pl.BlockSpec(memory_space=pltpu.SMEM)
@@ -41,15 +42,21 @@
     return high, mid, (rest - mid.astype(jnp.float32)).astype(jnp.bfloat16)
 
 
-def roll(trials, ids, dispatch_ref, bias, noise_ref):
+def inflow_of(ids, noise_ref):
     scenarios = lax.broadcasted_iota(jnp.int32, (noise_ref.shape[0] // 3, ids.shape[1]), 0)
     chosen = jnp.where(scenarios == ids, 1.0, 0.0)
     chosen = jnp.concatenate([chosen] * 3, axis=0).astype(jnp.bfloat16)
-    inflow = lax.dot_general(
+    return lax.dot_general(
         chosen, noise_ref[...], (((0,), (0,)), ((), ())), preferred_element_type=jnp.float32
     )
-    flow = jnp.dot(trials, dispatch_ref[...], preferred_element_type=jnp.float32)
-    return jnp.maximum(flow + bias + inflow, 0.0).astype(jnp.bfloat16)
+
+
+def flow_of(trials, dispatch_ref, bias):
+    return jnp.dot(trials, dispatch_ref[...], preferred_element_type=jnp.float32) + bias
+
+
+def next_of(flow, inflow):
+    return jnp.maximum(flow + inflow, 0.0).astype(jnp.bfloat16)
 
 
 def stage_kernel(
@@ -79,14 +86,19 @@
         column = jnp.broadcast_to(heights_ref[i : i + 1, :], (LANES, LANES)).T
         columns_ref[i * LANES : (i + 1) * LANES, :] = column
     copies[5].wait()
-    own_ref[...] = roll(trials_ref[...], ids_ref[...], dispatch_ref, bias_ref[...], noise3_ref)
+    flow = flow_of(trials_ref[...], dispatch_ref, bias_ref[...])
+    own_ref[...] = next_of(flow, inflow_of(ids_ref[...], noise3_ref))
     copies[6].wait()
 
 
-def roll_kernel(own_ref, other_ref, ids_ref, dispatch_ref, bias_ref, noise3_ref, out_ref):
+def flow_kernel(other_ref, dispatch_ref, bias_ref, flow_ref):
+    flow_ref[...] = flow_of(other_ref[...], dispatch_ref, bias_ref[...])
+
+
+def join_kernel(own_ref, flow_ref, ids_ref, noise3_ref, out_ref):
     rows = own_ref.shape[0]
     out_ref[0:rows, :] = own_ref[...]
-    out_ref[rows:, :] = roll(other_ref[...], ids_ref[...], dispatch_ref, bias_ref[...], noise3_ref)
+    out_ref[rows:, :] = next_of(flow_ref[...], inflow_of(ids_ref[...], noise3_ref))
 
 
 def sublane_top_two(first, second):
@@ -109,8 +121,7 @@
         piece, slot = pieces[i // held], i % held
         start = pl.multiple_of((me ^ offset) * rows, rows)
         states_ref[pl.ds(start, rows), :] = piece[slot * rows : (slot + 1) * rows, :]
-    count = counts_ref[0]
-    cuts, chunk = slopes_ref.shape[0], min(512, slopes_ref.shape[0])
+    cuts, chunk = slopes_ref.shape[0], min(256, slopes_ref.shape[0])
 
     def on_block(column):
         states = states_ref[pl.ds(column, block), :]
@@ -127,7 +138,7 @@
             here = here + jnp.concatenate([heights] * (block // LANES), axis=1)
             values_ref[start : start + chunk, pl.ds(column, block)] = here
             row = lax.broadcasted_iota(jnp.int32, (chunk, block), 0) + start
-            here = jnp.where(row < count, here, NEG)
+            here = jnp.where(row < counts_ref[0], here, NEG)
             for sub in range(0, chunk, 8):
                 v = here[sub : sub + 8]
                 second = jnp.maximum(second, jnp.minimum(first, v))
@@ -208,23 +219,34 @@
         ),
         name="stage",
     )(*(pltpu.with_memory_space_constraint(array, pltpu.HBM) for array in sources))
+    flow = pl.pallas_call(
+        flow_kernel,
+        out_shape=jax.ShapeDtypeStruct((rows, width), jnp.float32),
+        in_specs=[VMEM] * 3,
+        out_specs=VMEM,
+        compiler_params=pltpu.CompilerParams(vmem_limit_bytes=8 * MIB),
+        cost_estimate=pl.CostEstimate(
+            flops=2 * rows * width * width, bytes_accessed=2 * width * width, transcendentals=0
+        ),
+        name="flow",
+    )(other, dispatch, bias)
     held = pl.pallas_call(
-        roll_kernel,
+        join_kernel,
         out_shape=jax.ShapeDtypeStruct((2 * rows, width), jnp.bfloat16),
-        in_specs=[VMEM] * 6,
+        in_specs=[VMEM] * 4,
         out_specs=VMEM,
-        compiler_params=pltpu.CompilerParams(vmem_limit_bytes=16 * MIB),
-        cost_estimate=pl.CostEstimate(
-            flops=2 * rows * width * width, bytes_accessed=2 * width * width, transcendentals=0
-        ),
-        name="roll_forward",
-    )(own, other, other_ids, dispatch, bias, noise3)
+        compiler_params=pltpu.CompilerParams(vmem_limit_bytes=8 * MIB),
+        cost_estimate=pl.CostEstimate(
+            flops=6 * rows * scenarios * width, bytes_accessed=8 * rows * width, transcendentals=0
+        ),
+        name="inflow_join",
+    )(own, flow, other_ids, noise3)
     offsets = [0, steps[0]]
     for step in steps[1:]:
         held = jnp.concatenate([held, swap(held, step)], axis=0)
         offsets = offsets + [offset ^ step for offset in offsets]
-    pieces = [held] + [swap(held, step) for step in LAST]
-    offsets = [offset ^ step for step in (0, *LAST) for offset in offsets]
+    pieces = [held] + [swap(held, step) for step in NEAR_STATES]
+    offsets = [offset ^ step for step in (0, *NEAR_STATES) for offset in offsets]
 
     values, tops = pl.pallas_call(
         functools.partial(values_kernel, offsets, min(256, half)),
@@ -242,9 +264,12 @@
         name="cut_values",
     )(active_counts, slopes, heights, *pieces)
 
-    for step in steps:
+    for step in steps[:-1]:
         tops = merge(tops, swap(tops, step))
-    sets = [tops] + [swap(tops, step) for step in LAST]
+    far = steps[-1]
+    sets = [swap(tops, far * bit ^ near) for bit, near in ((1, 0), *EARLY_TOPS)]
+    tops = merge(tops, sets[0])
+    sets = [tops, *sets[1:], *(swap(tops, step) for step in LATE_TOPS)]
 
     chunk = min(256, cuts)
     return pl.pallas_call(

time: 31.6 us -> 30.1 us (0.953)
  waiting for transfers between devices: 11.5 us -> 8.28 us
  starting transfers between devices: 13 us -> 14.6 us
    ppermute x9 -> x10, waiting for transfers between devices: 11.5 us -> 8.28 us  [swap(): return lax.ppermute(array, 'cuts', [(i, i ^ step) for i in range(n)])]
    ppermute x9 -> x10, starting transfers between devices: 13 us -> 14.6 us  [swap(): return lax.ppermute(array, 'cuts', [(i, i ^ step) for i in range(n)])]
    pallas_call x1 -> x2, Pallas kernels: 0.57 us -> 0.66 us  [the longest x1 0.46 us: on_device(): pl.pallas_call(flow_kernel, out_shape=jax.ShapeDtypeStruct((rows, width),...]
  transfers between devices with their start and end apart: 9 -> 10, of which waited for: 8 -> 9; matrix products, arithmetic and copies ran while one was open for 0% -> 0% of each run, Pallas kernels for 10% -> 12%
where the time goes in v2:
time: 30.1 us; the launch traced here: 29.9 us
  starting transfers between devices  14.6 us (49%)
  waiting for transfers between devices  8.28 us (28%)
  Pallas kernels  6.28 us (21%)
  between operations  0.68 us (2%)
    ppermute x10, starting transfers between devices, swap(): return lax.ppermute(array, 'cuts', [(i, i ^ step) for i in range(n)])  14.6 us
    ppermute x10, waiting for transfers between devices, swap(): return lax.ppermute(array, 'cuts', [(i, i ^ step) for i in range(n)])  8.28 us
    pallas_call x1, Pallas kernels, on_device(): pl.pallas_call(stage_kernel, out_shape=(jax.ShapeDtypeStruct((rows, width...  3.06 us
    pallas_call x1, Pallas kernels, on_device(): pl.pallas_call(functools.partial(values_kernel, offsets, min(256, half)),...  1.44 us
    pallas_call x1, Pallas kernels, on_device(): pl.pallas_call(functools.partial(margins_kernel, chunk), out_shape=jax.Sh...  1.12 us
  transfers between devices with their start and end apart: 10, of which 9 were waited for; matrix products, arithmetic and copies ran while one was open for 0% of the time, Pallas kernels for 12%

profile of v2, /device:TPU:0, one launch (start us, length us, event | category | flops | bytes accessed | tf_op | source)
XLA Modules:
  0.0 29.9 jit_solution(8331697018709052746)
XLA Ops:
  0.0 4.0 %collective-permute-start = (bf16[32,1024]{1,0:T(8,128)(2,1)}, bf16[32,1024]{1,0:T(8,128)(2,1)S(1)}, u32[]{:S(2)}, u32[]{:S(2)}) collective-permute-start(bf16[32,1024]{1,0:T(8,128)(2,1)} %bitcast.3), channel_id=1, source_target_pairs={{0,8},{2,10},{4,12},{6,14},{8,0},{10,2},{12,4},{14,6},{1,9},{3,11}... | collective-permute-start | bytes 196616 | tf_op jit(solution)/shard_map/ppermute | solution.py:22
  4.0 0.0 collective-permute-start.1
  4.1 3.1 %stage.1 = (bf16[32,1024]{1,0:T(8,128)(2,1)S(1)}, bf16[1024,1024]{1,0:T(8,128)(2,1)S(1)}, f32[1,1024]{1,0:T(1,128)S(1)}, bf16[192,1024]{1,0:T(8,128)(2,1)S(1)}, ...) custom-call(bf16[32,1024]{1,0:T(8,128)(2,1)} %bitcast.4, s32[1,32]{1,0:T(1,128)} %ids_hbm.1, ...), custom_call_target="tpu_custom_call" | custom-call | flops 67108864 | bytes 6291456 | tf_op jit(solution)/shard_map/stage/pallas_call | solution.py:195
  7.1 0.8 %collective-permute-done.other_ref = bf16[32,1024]{1,0:T(8,128)(2,1)S(1)} collective-permute-done((bf16[32,1024]{1,0:T(8,128)(2,1)}, bf16[32,1024]{1,0:T(8,128)(2,1)S(1)}, u32[]{:S(2)}, u32[]{:S(2)}) %collective-permute-start) | collective-permute-done | bytes 65568 | tf_op jit(solution)/shard_map/ppermute | solution.py:22
  7.9 0.5 %flow.1.flow_ref = f32[32,1024]{1,0:T(8,128)S(1)} custom-call(bf16[32,1024]{1,0:T(8,128)(2,1)S(1)} %collective-permute-done.other_ref, bf16[1024,1024]{1,0:T(8,128)(2,1)S(1)} %get-tuple-element.16.dispatch_ref, f32[1,1024]{1,0:T(1,128)S(1)} %get-tuple-element.17.bias_ref), custom_call_target="tpu_custom_call" | custom-call | flops 67108864 | bytes 2097152 | tf_op jit(solution)/shard_map/flow/pallas_call | solution.py:222
  8.4 0.3 collective-permute-done.1.ids_ref
  8.6 0.2 inflow_join.1.refs_3_
  8.8 2.6 %collective-permute-start.2 = (bf16[64,1024]{1,0:T(8,128)(2,1)S(1)}, bf16[64,1024]{1,0:T(8,128)(2,1)S(1)}, u32[]{:S(2)}, u32[]{:S(2)}) collective-permute-start(bf16[64,1024]{1,0:T(8,128)(2,1)S(1)} %inflow_join.1.refs_3_), channel_id=1, source_target_pairs={{0,6},{2,4},{4,2},{6,0},{8,14},{10,12},{12,10},{14,8},{1,7},{3,5},... | collective-permute-start | bytes 393224 | tf_op jit(solution)/shard_map/ppermute | solution.py:22
  11.4 0.5 %collective-permute-start.3 = (bf16[64,1024]{1,0:T(8,128)(2,1)S(1)}, bf16[64,1024]{1,0:T(8,128)(2,1)S(1)}, u32[]{:S(2)}, u32[]{:S(2)}) collective-permute-start(bf16[64,1024]{1,0:T(8,128)(2,1)S(1)} %inflow_join.1.refs_3_), channel_id=1, source_target_pairs={{0,2},{2,0},{4,6},{6,4},{8,10},{10,8},{12,14},{14,12},{1,3},{3,1},... | collective-permute-start | bytes 393224 | tf_op jit(solution)/shard_map/ppermute | solution.py:22
  11.9 0.4 %collective-permute-start.4 = (bf16[64,1024]{1,0:T(8,128)(2,1)S(1)}, bf16[64,1024]{1,0:T(8,128)(2,1)S(1)}, u32[]{:S(2)}, u32[]{:S(2)}) collective-permute-start(bf16[64,1024]{1,0:T(8,128)(2,1)S(1)} %inflow_join.1.refs_3_), channel_id=1, source_target_pairs={{0,4},{2,6},{4,0},{6,2},{8,12},{10,14},{12,8},{14,10},{1,5},{3,7},... | collective-permute-start | bytes 393224 | tf_op jit(solution)/shard_map/ppermute | solution.py:22
  13.0 3.0 %collective-permute-done.2.refs_4_ = bf16[64,1024]{1,0:T(8,128)(2,1)S(1)} collective-permute-done((bf16[64,1024]{1,0:T(8,128)(2,1)S(1)}, bf16[64,1024]{1,0:T(8,128)(2,1)S(1)}, u32[]{:S(2)}, u32[]{:S(2)}) %collective-permute-start.2) | collective-permute-done | bytes 131104 | tf_op jit(solution)/shard_map/ppermute | solution.py:22
  16.0 1.4 %collective-permute-done.3.refs_5_ = bf16[64,1024]{1,0:T(8,128)(2,1)S(1)} collective-permute-done((bf16[64,1024]{1,0:T(8,128)(2,1)S(1)}, bf16[64,1024]{1,0:T(8,128)(2,1)S(1)}, u32[]{:S(2)}, u32[]{:S(2)}) %collective-permute-start.3) | collective-permute-done | bytes 131104 | tf_op jit(solution)/shard_map/ppermute | solution.py:22
  17.4 0.1 collective-permute-done.4.refs_6_
  17.4 1.4 %cut_values.1 = (f32[2048,256]{1,0:T(8,128)S(1)}, f32[2,256]{1,0:T(2,128)S(1)}) custom-call(s32[1]{0:T(128)S(6)} %copy.9.refs_0_.counts_ref, bf16[2048,1024]{1,0:T(8,128)(2,1)S(1)} %get-tuple-element.13.refs_1_, f32[2048,128]{1,0:T(8,128)S(1)} %get-tuple-element.14.refs_2_, bf16[64,1024]{1,0:T(8,128)(2,1)S(1)} %inflow_join.1.refs_3_, ...), custom_call_target="tpu_custom_call" | custom-call | flops 1073741824 | bytes 4194304 | tf_op jit(solution)/shard_map/cut_values/pallas_call | solution.py:251
  18.9 2.4 %collective-permute-start.5 = (f32[2,256]{1,0:T(2,128)S(1)}, f32[2,256]{1,0:T(2,128)S(1)}, u32[]{:S(2)}, u32[]{:S(2)}) collective-permute-start(f32[2,256]{1,0:T(2,128)S(1)} %get-tuple-element.20), channel_id=1, source_target_pairs={{0,8},{2,10},{4,12},{6,14},{8,0},{10,2},{12,4},{14,6},{1,9},{3,11}... | collective-permute-start | bytes 6152 | tf_op jit(solution)/shard_map/ppermute | solution.py:22
  21.2 1.1 %collective-permute-start.6 = (f32[2,256]{1,0:T(2,128)S(1)}, f32[2,256]{1,0:T(2,128)S(1)}, u32[]{:S(2)}, u32[]{:S(2)}) collective-permute-start(f32[2,256]{1,0:T(2,128)S(1)} %get-tuple-element.20), channel_id=1, source_target_pairs={{0,10},{2,8},{4,14},{6,12},{8,2},{10,0},{12,6},{14,4},{1,11},{3,9}... | collective-permute-start | bytes 6152 | tf_op jit(solution)/shard_map/ppermute | solution.py:22
  22.3 1.0 %collective-permute-start.7 = (f32[2,256]{1,0:T(2,128)S(1)}, f32[2,256]{1,0:T(2,128)S(1)}, u32[]{:S(2)}, u32[]{:S(2)}) collective-permute-start(f32[2,256]{1,0:T(2,128)S(1)} %get-tuple-element.20), channel_id=1, source_target_pairs={{0,2},{2,0},{4,6},{6,4},{8,10},{10,8},{12,14},{14,12},{1,3},{3,1},... | collective-permute-start | bytes 6152 | tf_op jit(solution)/shard_map/ppermute | solution.py:22
  23.3 0.1 collective-permute-done.5
  23.4 1.8 %collective-permute-start.8 = (f32[2,256]{1,0:T(2,128)S(1)}, f32[2,256]{1,0:T(2,128)S(1)}, u32[]{:S(2)}, u32[]{:S(2)}) collective-permute-start(f32[2,256]{1,0:T(2,128)S(1)} %pad_maximum_fusion.refs_0_), channel_id=1, source_target_pairs={{0,6},{2,4},{4,2},{6,0},{8,14},{10,12},{12,10},{14,8},{1,7},{3,5},... | collective-permute-start | bytes 6152 | tf_op jit(solution)/shard_map/ppermute | solution.py:22
  25.2 0.8 %collective-permute-start.9 = (f32[2,256]{1,0:T(2,128)S(1)}, f32[2,256]{1,0:T(2,128)S(1)}, u32[]{:S(2)}, u32[]{:S(2)}) collective-permute-start(f32[2,256]{1,0:T(2,128)S(1)} %pad_maximum_fusion.refs_0_), channel_id=1, source_target_pairs={{0,4},{2,6},{4,0},{6,2},{8,12},{10,14},{12,8},{14,10},{1,5},{3,7},... | collective-permute-start | bytes 6152 | tf_op jit(solution)/shard_map/ppermute | solution.py:22
  26.0 0.6 %collective-permute-done.6.refs_1_ = f32[2,256]{1,0:T(2,128)S(1)} collective-permute-done((f32[2,256]{1,0:T(2,128)S(1)}, f32[2,256]{1,0:T(2,128)S(1)}, u32[]{:S(2)}, u32[]{:S(2)}) %collective-permute-start.6) | collective-permute-done | bytes 2080 | tf_op jit(solution)/shard_map/ppermute | solution.py:22
  26.6 0.0 collective-permute-done.7.refs_2_
  26.6 1.4 %collective-permute-done.8.refs_3_ = f32[2,256]{1,0:T(2,128)S(1)} collective-permute-done((f32[2,256]{1,0:T(2,128)S(1)}, f32[2,256]{1,0:T(2,128)S(1)}, u32[]{:S(2)}, u32[]{:S(2)}) %collective-permute-start.8) | collective-permute-done | bytes 2080 | tf_op jit(solution)/shard_map/ppermute | solution.py:22
  28.0 0.8 %collective-permute-done.9.refs_4_ = f32[2,256]{1,0:T(2,128)S(1)} collective-permute-done((f32[2,256]{1,0:T(2,128)S(1)}, f32[2,256]{1,0:T(2,128)S(1)}, u32[]{:S(2)}, u32[]{:S(2)}) %collective-permute-start.9) | collective-permute-done | bytes 2080 | tf_op jit(solution)/shard_map/ppermute | solution.py:22
  28.8 1.1 %margins.1 = bf16[2048,256]{1,0:T(8,128)(2,1)} custom-call(s32[1]{0:T(128)S(6)} %copy.9.refs_0_.counts_ref, f32[2048,256]{1,0:T(8,128)S(1)} %get-tuple-element.19.values_ref, f32[2,256]{1,0:T(2,128)S(1)} %pad_maximum_fusion.refs_0_, f32[2,256]{1,0:T(2,128)S(1)} %collective-permute-done.6.refs_1_, f32[2,256]{1,0:T(2,128)S(1)} %collective-permute-done.7.refs_2_, ...), custom_call_target="tpu_custom_call" | custom-call | flops 2097152 | bytes 1048576 | tf_op jit(solution)/shard_map/margins/pallas_call | solution.py:275
  (2 shorter events, 0.0 us)
Async XLA Ops:
  0.0 7.9 %collective-permute-start = (bf16[32,1024]{1,0:T(8,128)(2,1)}, bf16[32,1024]{1,0:T(8,128)(2,1)S(1)}, u32[]{:S(2)}, u32[]{:S(2)}) collective-permute-start(bf16[32,1024]{1,0:T(8,128)(2,1)} %bitcast.3), channel_id=1, source_target_pairs={{0,8},{2,10},{4,12},{6,14},{8,0},{10,2},{12,4},{14,6},{1,9},{3,11}... | collective-permute-start | bytes 196616 | tf_op jit(solution)/shard_map/ppermute | solution.py:22
  4.0 4.6 %collective-permute-start.1 = (s32[1,32]{1,0:T(1,128)}, s32[1,32]{1,0:T(1,128)S(1)}, u32[]{:S(2)}, u32[]{:S(2)}) collective-permute-start(s32[1,32]{1,0:T(1,128)} %ids_hbm.1), channel_id=1, source_target_pairs={{0,8},{2,10},{4,12},{6,14},{8,0},{10,2},{12,4},{14,6},{1,9},{3,11}... | collective-permute-start | bytes 392 | tf_op jit(solution)/shard_map/ppermute | solution.py:22
  8.8 7.2 %collective-permute-start.2 = (bf16[64,1024]{1,0:T(8,128)(2,1)S(1)}, bf16[64,1024]{1,0:T(8,128)(2,1)S(1)}, u32[]{:S(2)}, u32[]{:S(2)}) collective-permute-start(bf16[64,1024]{1,0:T(8,128)(2,1)S(1)} %inflow_join.1.refs_3_), channel_id=1, source_target_pairs={{0,6},{2,4},{4,2},{6,0},{8,14},{10,12},{12,10},{14,8},{1,7},{3,5},... | collective-permute-start | bytes 393224 | tf_op jit(solution)/shard_map/ppermute | solution.py:22
  11.4 6.0 %collective-permute-start.3 = (bf16[64,1024]{1,0:T(8,128)(2,1)S(1)}, bf16[64,1024]{1,0:T(8,128)(2,1)S(1)}, u32[]{:S(2)}, u32[]{:S(2)}) collective-permute-start(bf16[64,1024]{1,0:T(8,128)(2,1)S(1)} %inflow_join.1.refs_3_), channel_id=1, source_target_pairs={{0,2},{2,0},{4,6},{6,4},{8,10},{10,8},{12,14},{14,12},{1,3},{3,1},... | collective-permute-start | bytes 393224 | tf_op jit(solution)/shard_map/ppermute | solution.py:22
  11.9 5.5 %collective-permute-start.4 = (bf16[64,1024]{1,0:T(8,128)(2,1)S(1)}, bf16[64,1024]{1,0:T(8,128)(2,1)S(1)}, u32[]{:S(2)}, u32[]{:S(2)}) collective-permute-start(bf16[64,1024]{1,0:T(8,128)(2,1)S(1)} %inflow_join.1.refs_3_), channel_id=1, source_target_pairs={{0,4},{2,6},{4,0},{6,2},{8,12},{10,14},{12,8},{14,10},{1,5},{3,7},... | collective-permute-start | bytes 393224 | tf_op jit(solution)/shard_map/ppermute | solution.py:22
  18.9 4.5 %collective-permute-start.5 = (f32[2,256]{1,0:T(2,128)S(1)}, f32[2,256]{1,0:T(2,128)S(1)}, u32[]{:S(2)}, u32[]{:S(2)}) collective-permute-start(f32[2,256]{1,0:T(2,128)S(1)} %get-tuple-element.20), channel_id=1, source_target_pairs={{0,8},{2,10},{4,12},{6,14},{8,0},{10,2},{12,4},{14,6},{1,9},{3,11}... | collective-permute-start | bytes 6152 | tf_op jit(solution)/shard_map/ppermute | solution.py:22
  21.2 5.4 %collective-permute-start.6 = (f32[2,256]{1,0:T(2,128)S(1)}, f32[2,256]{1,0:T(2,128)S(1)}, u32[]{:S(2)}, u32[]{:S(2)}) collective-permute-start(f32[2,256]{1,0:T(2,128)S(1)} %get-tuple-element.20), channel_id=1, source_target_pairs={{0,10},{2,8},{4,14},{6,12},{8,2},{10,0},{12,6},{14,4},{1,11},{3,9}... | collective-permute-start | bytes 6152 | tf_op jit(solution)/shard_map/ppermute | solution.py:22
  22.3 4.3 %collective-permute-start.7 = (f32[2,256]{1,0:T(2,128)S(1)}, f32[2,256]{1,0:T(2,128)S(1)}, u32[]{:S(2)}, u32[]{:S(2)}) collective-permute-start(f32[2,256]{1,0:T(2,128)S(1)} %get-tuple-element.20), channel_id=1, source_target_pairs={{0,2},{2,0},{4,6},{6,4},{8,10},{10,8},{12,14},{14,12},{1,3},{3,1},... | collective-permute-start | bytes 6152 | tf_op jit(solution)/shard_map/ppermute | solution.py:22
  23.4 4.5 %collective-permute-start.8 = (f32[2,256]{1,0:T(2,128)S(1)}, f32[2,256]{1,0:T(2,128)S(1)}, u32[]{:S(2)}, u32[]{:S(2)}) collective-permute-start(f32[2,256]{1,0:T(2,128)S(1)} %pad_maximum_fusion.refs_0_), channel_id=1, source_target_pairs={{0,6},{2,4},{4,2},{6,0},{8,14},{10,12},{12,10},{14,8},{1,7},{3,5},... | collective-permute-start | bytes 6152 | tf_op jit(solution)/shard_map/ppermute | solution.py:22
  25.2 3.6 %collective-permute-start.9 = (f32[2,256]{1,0:T(2,128)S(1)}, f32[2,256]{1,0:T(2,128)S(1)}, u32[]{:S(2)}, u32[]{:S(2)}) collective-permute-start(f32[2,256]{1,0:T(2,128)S(1)} %pad_maximum_fusion.refs_0_), channel_id=1, source_target_pairs={{0,4},{2,6},{4,0},{6,2},{8,12},{10,14},{12,8},{14,10},{1,5},{3,7},... | collective-permute-start | bytes 6152 | tf_op jit(solution)/shard_map/ppermute | solution.py:22

commit v3 on v2

--- a/solution.py
+++ b/solution.py
@@ -11,7 +11,7 @@
 MIB = 1024 * 1024
 LANES = 128
 NEAR_STATES = (3, 1, 2)
-EARLY_TOPS, LATE_TOPS = ((1, 1), (0, 1)), (3, 2)
+EARLY_TOPS, LATE_TOPS = ((0, 1), (1, 1)), (3, 2)
 VMEM = pl.BlockSpec(memory_space=pltpu.VMEM)
 HBM = pl.BlockSpec(memory_space=pltpu.HBM)
 SMEM = pl.BlockSpec(memory_space=pltpu.SMEM)
@@ -134,11 +134,10 @@
                 (((1,), (1,)), ((), ())),
                 preferred_element_type=jnp.float32,
             )
-            heights = heights_ref[start : start + chunk, :]
+            row = lax.broadcasted_iota(jnp.int32, (chunk, LANES), 0) + start
+            heights = jnp.where(row < counts_ref[0], heights_ref[start : start + chunk, :], NEG)
             here = here + jnp.concatenate([heights] * (block // LANES), axis=1)
             values_ref[start : start + chunk, pl.ds(column, block)] = here
-            row = lax.broadcasted_iota(jnp.int32, (chunk, block), 0) + start
-            here = jnp.where(row < counts_ref[0], here, NEG)
             for sub in range(0, chunk, 8):
                 v = here[sub : sub + 8]
                 second = jnp.maximum(second, jnp.minimum(first, v))

time: 30.1 us -> 30 us (level)
  no operation moved by 1% of the time
where the time goes in v3:
time: 30 us; the launch traced here: 29.9 us
  starting transfers between devices  14.6 us (49%)
  waiting for transfers between devices  8.28 us (28%)
  Pallas kernels  6.26 us (21%)
  between operations  0.68 us (2%)
    ppermute x10, starting transfers between devices, swap(): return lax.ppermute(array, 'cuts', [(i, i ^ step) for i in range(n)])  14.6 us
    ppermute x10, waiting for transfers between devices, swap(): return lax.ppermute(array, 'cuts', [(i, i ^ step) for i in range(n)])  8.28 us
    pallas_call x1, Pallas kernels, on_device(): pl.pallas_call(stage_kernel, out_shape=(jax.ShapeDtypeStruct((rows, width...  3.06 us
    pallas_call x1, Pallas kernels, on_device(): pl.pallas_call(functools.partial(values_kernel, offsets, min(256, half)),...  1.41 us
    pallas_call x1, Pallas kernels, on_device(): pl.pallas_call(functools.partial(margins_kernel, chunk), out_shape=jax.Sh...  1.12 us
  transfers between devices with their start and end apart: 10, of which 9 were waited for; matrix products, arithmetic and copies ran while one was open for 0% of the time, Pallas kernels for 12%

profile of v3, /device:TPU:0, one launch (start us, length us, event | category | flops | bytes accessed | tf_op | source)
XLA Modules:
  0.0 29.9 jit_solution(17015786103765641013)
XLA Ops:
  0.0 4.0 %collective-permute-start = (bf16[32,1024]{1,0:T(8,128)(2,1)}, bf16[32,1024]{1,0:T(8,128)(2,1)S(1)}, u32[]{:S(2)}, u32[]{:S(2)}) collective-permute-start(bf16[32,1024]{1,0:T(8,128)(2,1)} %bitcast.3), channel_id=1, source_target_pairs={{0,8},{2,10},{4,12},{6,14},{8,0},{10,2},{12,4},{14,6},{1,9},{3,11}... | collective-permute-start | bytes 196616 | tf_op jit(solution)/shard_map/ppermute | solution.py:22
  4.0 0.0 collective-permute-start.1
  4.1 3.1 %stage.1 = (bf16[32,1024]{1,0:T(8,128)(2,1)S(1)}, bf16[1024,1024]{1,0:T(8,128)(2,1)S(1)}, f32[1,1024]{1,0:T(1,128)S(1)}, bf16[192,1024]{1,0:T(8,128)(2,1)S(1)}, ...) custom-call(bf16[32,1024]{1,0:T(8,128)(2,1)} %bitcast.4, s32[1,32]{1,0:T(1,128)} %ids_hbm.1, ...), custom_call_target="tpu_custom_call" | custom-call | flops 67108864 | bytes 6291456 | tf_op jit(solution)/shard_map/stage/pallas_call | solution.py:194
  7.1 0.8 %collective-permute-done.other_ref = bf16[32,1024]{1,0:T(8,128)(2,1)S(1)} collective-permute-done((bf16[32,1024]{1,0:T(8,128)(2,1)}, bf16[32,1024]{1,0:T(8,128)(2,1)S(1)}, u32[]{:S(2)}, u32[]{:S(2)}) %collective-permute-start) | collective-permute-done | bytes 65568 | tf_op jit(solution)/shard_map/ppermute | solution.py:22
  7.9 0.5 %flow.1.flow_ref = f32[32,1024]{1,0:T(8,128)S(1)} custom-call(bf16[32,1024]{1,0:T(8,128)(2,1)S(1)} %collective-permute-done.other_ref, bf16[1024,1024]{1,0:T(8,128)(2,1)S(1)} %get-tuple-element.16.dispatch_ref, f32[1,1024]{1,0:T(1,128)S(1)} %get-tuple-element.17.bias_ref), custom_call_target="tpu_custom_call" | custom-call | flops 67108864 | bytes 2097152 | tf_op jit(solution)/shard_map/flow/pallas_call | solution.py:221
  8.4 0.3 collective-permute-done.1.ids_ref
  8.6 0.2 inflow_join.1.refs_3_
  8.8 2.6 %collective-permute-start.2 = (bf16[64,1024]{1,0:T(8,128)(2,1)S(1)}, bf16[64,1024]{1,0:T(8,128)(2,1)S(1)}, u32[]{:S(2)}, u32[]{:S(2)}) collective-permute-start(bf16[64,1024]{1,0:T(8,128)(2,1)S(1)} %inflow_join.1.refs_3_), channel_id=1, source_target_pairs={{0,6},{2,4},{4,2},{6,0},{8,14},{10,12},{12,10},{14,8},{1,7},{3,5},... | collective-permute-start | bytes 393224 | tf_op jit(solution)/shard_map/ppermute | solution.py:22
  11.4 0.5 %collective-permute-start.3 = (bf16[64,1024]{1,0:T(8,128)(2,1)S(1)}, bf16[64,1024]{1,0:T(8,128)(2,1)S(1)}, u32[]{:S(2)}, u32[]{:S(2)}) collective-permute-start(bf16[64,1024]{1,0:T(8,128)(2,1)S(1)} %inflow_join.1.refs_3_), channel_id=1, source_target_pairs={{0,2},{2,0},{4,6},{6,4},{8,10},{10,8},{12,14},{14,12},{1,3},{3,1},... | collective-permute-start | bytes 393224 | tf_op jit(solution)/shard_map/ppermute | solution.py:22
  11.9 0.4 %collective-permute-start.4 = (bf16[64,1024]{1,0:T(8,128)(2,1)S(1)}, bf16[64,1024]{1,0:T(8,128)(2,1)S(1)}, u32[]{:S(2)}, u32[]{:S(2)}) collective-permute-start(bf16[64,1024]{1,0:T(8,128)(2,1)S(1)} %inflow_join.1.refs_3_), channel_id=1, source_target_pairs={{0,4},{2,6},{4,0},{6,2},{8,12},{10,14},{12,8},{14,10},{1,5},{3,7},... | collective-permute-start | bytes 393224 | tf_op jit(solution)/shard_map/ppermute | solution.py:22
  13.0 3.0 %collective-permute-done.2.refs_4_ = bf16[64,1024]{1,0:T(8,128)(2,1)S(1)} collective-permute-done((bf16[64,1024]{1,0:T(8,128)(2,1)S(1)}, bf16[64,1024]{1,0:T(8,128)(2,1)S(1)}, u32[]{:S(2)}, u32[]{:S(2)}) %collective-permute-start.2) | collective-permute-done | bytes 131104 | tf_op jit(solution)/shard_map/ppermute | solution.py:22
  16.0 1.4 %collective-permute-done.3.refs_5_ = bf16[64,1024]{1,0:T(8,128)(2,1)S(1)} collective-permute-done((bf16[64,1024]{1,0:T(8,128)(2,1)S(1)}, bf16[64,1024]{1,0:T(8,128)(2,1)S(1)}, u32[]{:S(2)}, u32[]{:S(2)}) %collective-permute-start.3) | collective-permute-done | bytes 131104 | tf_op jit(solution)/shard_map/ppermute | solution.py:22
  17.4 0.1 collective-permute-done.4.refs_6_
  17.4 1.4 %cut_values.1 = (f32[2048,256]{1,0:T(8,128)S(1)}, f32[2,256]{1,0:T(2,128)S(1)}) custom-call(s32[1]{0:T(128)S(6)} %copy.9.refs_0_.counts_ref, bf16[2048,1024]{1,0:T(8,128)(2,1)S(1)} %get-tuple-element.13.refs_1_, f32[2048,128]{1,0:T(8,128)S(1)} %get-tuple-element.14.refs_2_, bf16[64,1024]{1,0:T(8,128)(2,1)S(1)} %inflow_join.1.refs_3_, ...), custom_call_target="tpu_custom_call" | custom-call | flops 1073741824 | bytes 4194304 | tf_op jit(solution)/shard_map/cut_values/pallas_call | solution.py:250
  18.8 2.4 %collective-permute-start.5 = (f32[2,256]{1,0:T(2,128)S(1)}, f32[2,256]{1,0:T(2,128)S(1)}, u32[]{:S(2)}, u32[]{:S(2)}) collective-permute-start(f32[2,256]{1,0:T(2,128)S(1)} %get-tuple-element.20), channel_id=1, source_target_pairs={{0,8},{2,10},{4,12},{6,14},{8,0},{10,2},{12,4},{14,6},{1,9},{3,11}... | collective-permute-start | bytes 6152 | tf_op jit(solution)/shard_map/ppermute | solution.py:22
  21.2 1.0 %collective-permute-start.6 = (f32[2,256]{1,0:T(2,128)S(1)}, f32[2,256]{1,0:T(2,128)S(1)}, u32[]{:S(2)}, u32[]{:S(2)}) collective-permute-start(f32[2,256]{1,0:T(2,128)S(1)} %get-tuple-element.20), channel_id=1, source_target_pairs={{0,2},{2,0},{4,6},{6,4},{8,10},{10,8},{12,14},{14,12},{1,3},{3,1},... | collective-permute-start | bytes 6152 | tf_op jit(solution)/shard_map/ppermute | solution.py:22
  22.2 1.1 %collective-permute-start.7 = (f32[2,256]{1,0:T(2,128)S(1)}, f32[2,256]{1,0:T(2,128)S(1)}, u32[]{:S(2)}, u32[]{:S(2)}) collective-permute-start(f32[2,256]{1,0:T(2,128)S(1)} %get-tuple-element.20), channel_id=1, source_target_pairs={{0,10},{2,8},{4,14},{6,12},{8,2},{10,0},{12,6},{14,4},{1,11},{3,9}... | collective-permute-start | bytes 6152 | tf_op jit(solution)/shard_map/ppermute | solution.py:22
  23.3 0.1 collective-permute-done.5
  23.4 1.8 %collective-permute-start.8 = (f32[2,256]{1,0:T(2,128)S(1)}, f32[2,256]{1,0:T(2,128)S(1)}, u32[]{:S(2)}, u32[]{:S(2)}) collective-permute-start(f32[2,256]{1,0:T(2,128)S(1)} %pad_maximum_fusion.refs_0_), channel_id=1, source_target_pairs={{0,6},{2,4},{4,2},{6,0},{8,14},{10,12},{12,10},{14,8},{1,7},{3,5},... | collective-permute-start | bytes 6152 | tf_op jit(solution)/shard_map/ppermute | solution.py:22
  25.2 0.8 %collective-permute-start.9 = (f32[2,256]{1,0:T(2,128)S(1)}, f32[2,256]{1,0:T(2,128)S(1)}, u32[]{:S(2)}, u32[]{:S(2)}) collective-permute-start(f32[2,256]{1,0:T(2,128)S(1)} %pad_maximum_fusion.refs_0_), channel_id=1, source_target_pairs={{0,4},{2,6},{4,0},{6,2},{8,12},{10,14},{12,8},{14,10},{1,5},{3,7},... | collective-permute-start | bytes 6152 | tf_op jit(solution)/shard_map/ppermute | solution.py:22
  26.0 0.0 collective-permute-done.6.refs_1_
  26.0 1.6 %collective-permute-done.7.refs_2_ = f32[2,256]{1,0:T(2,128)S(1)} collective-permute-done((f32[2,256]{1,0:T(2,128)S(1)}, f32[2,256]{1,0:T(2,128)S(1)}, u32[]{:S(2)}, u32[]{:S(2)}) %collective-permute-start.7) | collective-permute-done | bytes 2080 | tf_op jit(solution)/shard_map/ppermute | solution.py:22
  27.6 0.4 %collective-permute-done.8.refs_3_ = f32[2,256]{1,0:T(2,128)S(1)} collective-permute-done((f32[2,256]{1,0:T(2,128)S(1)}, f32[2,256]{1,0:T(2,128)S(1)}, u32[]{:S(2)}, u32[]{:S(2)}) %collective-permute-start.8) | collective-permute-done | bytes 2080 | tf_op jit(solution)/shard_map/ppermute | solution.py:22
  28.0 0.8 %collective-permute-done.9.refs_4_ = f32[2,256]{1,0:T(2,128)S(1)} collective-permute-done((f32[2,256]{1,0:T(2,128)S(1)}, f32[2,256]{1,0:T(2,128)S(1)}, u32[]{:S(2)}, u32[]{:S(2)}) %collective-permute-start.9) | collective-permute-done | bytes 2080 | tf_op jit(solution)/shard_map/ppermute | solution.py:22
  28.8 1.1 %margins.1 = bf16[2048,256]{1,0:T(8,128)(2,1)} custom-call(s32[1]{0:T(128)S(6)} %copy.9.refs_0_.counts_ref, f32[2048,256]{1,0:T(8,128)S(1)} %get-tuple-element.19.values_ref, f32[2,256]{1,0:T(2,128)S(1)} %pad_maximum_fusion.refs_0_, f32[2,256]{1,0:T(2,128)S(1)} %collective-permute-done.6.refs_1_, f32[2,256]{1,0:T(2,128)S(1)} %collective-permute-done.7.refs_2_, ...), custom_call_target="tpu_custom_call" | custom-call | flops 2097152 | bytes 1048576 | tf_op jit(solution)/shard_map/margins/pallas_call | solution.py:274
  (2 shorter events, 0.0 us)
Async XLA Ops:
  0.0 7.9 %collective-permute-start = (bf16[32,1024]{1,0:T(8,128)(2,1)}, bf16[32,1024]{1,0:T(8,128)(2,1)S(1)}, u32[]{:S(2)}, u32[]{:S(2)}) collective-permute-start(bf16[32,1024]{1,0:T(8,128)(2,1)} %bitcast.3), channel_id=1, source_target_pairs={{0,8},{2,10},{4,12},{6,14},{8,0},{10,2},{12,4},{14,6},{1,9},{3,11}... | collective-permute-start | bytes 196616 | tf_op jit(solution)/shard_map/ppermute | solution.py:22
  4.0 4.6 %collective-permute-start.1 = (s32[1,32]{1,0:T(1,128)}, s32[1,32]{1,0:T(1,128)S(1)}, u32[]{:S(2)}, u32[]{:S(2)}) collective-permute-start(s32[1,32]{1,0:T(1,128)} %ids_hbm.1), channel_id=1, source_target_pairs={{0,8},{2,10},{4,12},{6,14},{8,0},{10,2},{12,4},{14,6},{1,9},{3,11}... | collective-permute-start | bytes 392 | tf_op jit(solution)/shard_map/ppermute | solution.py:22
  8.8 7.2 %collective-permute-start.2 = (bf16[64,1024]{1,0:T(8,128)(2,1)S(1)}, bf16[64,1024]{1,0:T(8,128)(2,1)S(1)}, u32[]{:S(2)}, u32[]{:S(2)}) collective-permute-start(bf16[64,1024]{1,0:T(8,128)(2,1)S(1)} %inflow_join.1.refs_3_), channel_id=1, source_target_pairs={{0,6},{2,4},{4,2},{6,0},{8,14},{10,12},{12,10},{14,8},{1,7},{3,5},... | collective-permute-start | bytes 393224 | tf_op jit(solution)/shard_map/ppermute | solution.py:22
  11.4 6.0 %collective-permute-start.3 = (bf16[64,1024]{1,0:T(8,128)(2,1)S(1)}, bf16[64,1024]{1,0:T(8,128)(2,1)S(1)}, u32[]{:S(2)}, u32[]{:S(2)}) collective-permute-start(bf16[64,1024]{1,0:T(8,128)(2,1)S(1)} %inflow_join.1.refs_3_), channel_id=1, source_target_pairs={{0,2},{2,0},{4,6},{6,4},{8,10},{10,8},{12,14},{14,12},{1,3},{3,1},... | collective-permute-start | bytes 393224 | tf_op jit(solution)/shard_map/ppermute | solution.py:22
  11.9 5.5 %collective-permute-start.4 = (bf16[64,1024]{1,0:T(8,128)(2,1)S(1)}, bf16[64,1024]{1,0:T(8,128)(2,1)S(1)}, u32[]{:S(2)}, u32[]{:S(2)}) collective-permute-start(bf16[64,1024]{1,0:T(8,128)(2,1)S(1)} %inflow_join.1.refs_3_), channel_id=1, source_target_pairs={{0,4},{2,6},{4,0},{6,2},{8,12},{10,14},{12,8},{14,10},{1,5},{3,7},... | collective-permute-start | bytes 393224 | tf_op jit(solution)/shard_map/ppermute | solution.py:22
  18.8 4.5 %collective-permute-start.5 = (f32[2,256]{1,0:T(2,128)S(1)}, f32[2,256]{1,0:T(2,128)S(1)}, u32[]{:S(2)}, u32[]{:S(2)}) collective-permute-start(f32[2,256]{1,0:T(2,128)S(1)} %get-tuple-element.20), channel_id=1, source_target_pairs={{0,8},{2,10},{4,12},{6,14},{8,0},{10,2},{12,4},{14,6},{1,9},{3,11}... | collective-permute-start | bytes 6152 | tf_op jit(solution)/shard_map/ppermute | solution.py:22
  21.2 4.8 %collective-permute-start.6 = (f32[2,256]{1,0:T(2,128)S(1)}, f32[2,256]{1,0:T(2,128)S(1)}, u32[]{:S(2)}, u32[]{:S(2)}) collective-permute-start(f32[2,256]{1,0:T(2,128)S(1)} %get-tuple-element.20), channel_id=1, source_target_pairs={{0,2},{2,0},{4,6},{6,4},{8,10},{10,8},{12,14},{14,12},{1,3},{3,1},... | collective-permute-start | bytes 6152 | tf_op jit(solution)/shard_map/ppermute | solution.py:22
  22.2 5.4 %collective-permute-start.7 = (f32[2,256]{1,0:T(2,128)S(1)}, f32[2,256]{1,0:T(2,128)S(1)}, u32[]{:S(2)}, u32[]{:S(2)}) collective-permute-start(f32[2,256]{1,0:T(2,128)S(1)} %get-tuple-element.20), channel_id=1, source_target_pairs={{0,10},{2,8},{4,14},{6,12},{8,2},{10,0},{12,6},{14,4},{1,11},{3,9}... | collective-permute-start | bytes 6152 | tf_op jit(solution)/shard_map/ppermute | solution.py:22
  23.4 4.5 %collective-permute-start.8 = (f32[2,256]{1,0:T(2,128)S(1)}, f32[2,256]{1,0:T(2,128)S(1)}, u32[]{:S(2)}, u32[]{:S(2)}) collective-permute-start(f32[2,256]{1,0:T(2,128)S(1)} %pad_maximum_fusion.refs_0_), channel_id=1, source_target_pairs={{0,6},{2,4},{4,2},{6,0},{8,14},{10,12},{12,10},{14,8},{1,7},{3,5},... | collective-permute-start | bytes 6152 | tf_op jit(solution)/shard_map/ppermute | solution.py:22
  25.2 3.6 %collective-permute-start.9 = (f32[2,256]{1,0:T(2,128)S(1)}, f32[2,256]{1,0:T(2,128)S(1)}, u32[]{:S(2)}, u32[]{:S(2)}) collective-permute-start(f32[2,256]{1,0:T(2,128)S(1)} %pad_maximum_fusion.refs_0_), channel_id=1, source_target_pairs={{0,4},{2,6},{4,0},{6,2},{8,12},{10,14},{12,8},{14,10},{1,5},{3,7},... | collective-permute-start | bytes 6152 | tf_op jit(solution)/shard_map/ppermute | solution.py:22

commit v4 on v3

--- a/solution.py
+++ b/solution.py
@@ -20,6 +20,12 @@
 def swap(array, step):
     n = lax.axis_size("cuts")
     return lax.ppermute(array, "cuts", [(i, i ^ step) for i in range(n)])
+
+
+def cross(array, step):
+    n = lax.axis_size("cuts")
+    pairs = [(2 * i + core, 2 * (i ^ step) + 1 - core) for i in range(n) for core in range(2)]
+    return lax.ppermute(array, ("cuts", "states"), pairs)
 
 
 def early_steps(n):
@@ -266,9 +272,10 @@
     for step in steps[:-1]:
         tops = merge(tops, swap(tops, step))
     far = steps[-1]
-    sets = [swap(tops, far * bit ^ near) for bit, near in ((1, 0), *EARLY_TOPS)]
-    tops = merge(tops, sets[0])
-    sets = [tops, *sets[1:], *(swap(tops, step) for step in LATE_TOPS)]
+    mirror, met = cross(tops, 0), cross(tops, far)
+    early = [swap(tops, far * bit ^ near) for bit, near in EARLY_TOPS]
+    merged = merge(mirror, met)
+    sets = [cross(merged, 0), *early, *(cross(merged, step) for step in LATE_TOPS)]
 
     chunk = min(256, cuts)
     return pl.pallas_call(

time: 30 us -> 29.2 us (0.973)
  waiting for transfers between devices: 8.28 us -> 7.41 us
    ppermute x10 -> x7, starting transfers between devices: 14.6 us -> 9.72 us  [swap(): return lax.ppermute(array, 'cuts', [(i, i ^ step) for i in range(n)])]
    ppermute x0 -> x5, starting transfers between devices: none -> 4.77 us  [cross(): return lax.ppermute(array, ('cuts', 'states'), pairs)]
    ppermute x10 -> x7, waiting for transfers between devices: 8.28 us -> 7.36 us  [swap(): return lax.ppermute(array, 'cuts', [(i, i ^ step) for i in range(n)])]
  transfers between devices with their start and end apart: 10 -> 12, of which waited for: 9 -> 6; matrix products, arithmetic and copies ran while one was open for 0% -> 0% of each run, Pallas kernels for 12% -> 12%
where the time goes in v4:
time: 29.2 us; the launch traced here: 28.9 us
  starting transfers between devices  14.5 us (50%)
  waiting for transfers between devices  7.41 us (25%)
  Pallas kernels  6.26 us (21%)
  between operations  0.7 us (2%)
    ppermute x7, starting transfers between devices, swap(): return lax.ppermute(array, 'cuts', [(i, i ^ step) for i in range(n)])  9.72 us
    ppermute x7, waiting for transfers between devices, swap(): return lax.ppermute(array, 'cuts', [(i, i ^ step) for i in range(n)])  7.36 us
    ppermute x5, starting transfers between devices, cross(): return lax.ppermute(array, ('cuts', 'states'), pairs)  4.77 us
    pallas_call x1, Pallas kernels, on_device(): pl.pallas_call(stage_kernel, out_shape=(jax.ShapeDtypeStruct((rows, width...  3.06 us
    pallas_call x1, Pallas kernels, on_device(): pl.pallas_call(functools.partial(values_kernel, offsets, min(256, half)),...  1.41 us
    pallas_call x1, Pallas kernels, on_device(): pl.pallas_call(functools.partial(margins_kernel, chunk), out_shape=jax.Sh...  1.12 us
  transfers between devices with their start and end apart: 12, of which 6 were waited for; matrix products, arithmetic and copies ran while one was open for 0% of the time, Pallas kernels for 12%

profile of v4, /device:TPU:0, one launch (start us, length us, event | category | flops | bytes accessed | tf_op | source)
XLA Modules:
  0.0 28.9 jit_solution(9367703172002210510)
XLA Ops:
  0.0 4.0 %collective-permute-start = (bf16[32,1024]{1,0:T(8,128)(2,1)}, bf16[32,1024]{1,0:T(8,128)(2,1)S(1)}, u32[]{:S(2)}, u32[]{:S(2)}) collective-permute-start(bf16[32,1024]{1,0:T(8,128)(2,1)} %bitcast.3), channel_id=1, source_target_pairs={{0,8},{2,10},{4,12},{6,14},{8,0},{10,2},{12,4},{14,6},{1,9},{3,11}... | collective-permute-start | bytes 196616 | tf_op jit(solution)/shard_map/ppermute | solution.py:22
  4.0 0.0 collective-permute-start.1
  4.1 3.1 %stage.1 = (bf16[32,1024]{1,0:T(8,128)(2,1)S(1)}, bf16[1024,1024]{1,0:T(8,128)(2,1)S(1)}, f32[1,1024]{1,0:T(1,128)S(1)}, bf16[192,1024]{1,0:T(8,128)(2,1)S(1)}, ...) custom-call(bf16[32,1024]{1,0:T(8,128)(2,1)} %bitcast.4, s32[1,32]{1,0:T(1,128)} %ids_hbm.1, ...), custom_call_target="tpu_custom_call" | custom-call | flops 67108864 | bytes 6291456 | tf_op jit(solution)/shard_map/stage/pallas_call | solution.py:200
  7.1 0.8 %collective-permute-done.other_ref = bf16[32,1024]{1,0:T(8,128)(2,1)S(1)} collective-permute-done((bf16[32,1024]{1,0:T(8,128)(2,1)}, bf16[32,1024]{1,0:T(8,128)(2,1)S(1)}, u32[]{:S(2)}, u32[]{:S(2)}) %collective-permute-start) | collective-permute-done | bytes 65568 | tf_op jit(solution)/shard_map/ppermute | solution.py:22
  7.9 0.5 %flow.1.flow_ref = f32[32,1024]{1,0:T(8,128)S(1)} custom-call(bf16[32,1024]{1,0:T(8,128)(2,1)S(1)} %collective-permute-done.other_ref, bf16[1024,1024]{1,0:T(8,128)(2,1)S(1)} %get-tuple-element.16.dispatch_ref, f32[1,1024]{1,0:T(1,128)S(1)} %get-tuple-element.17.bias_ref), custom_call_target="tpu_custom_call" | custom-call | flops 67108864 | bytes 2097152 | tf_op jit(solution)/shard_map/flow/pallas_call | solution.py:227
  8.4 0.3 collective-permute-done.1.ids_ref
  8.6 0.2 inflow_join.1.refs_3_
  8.8 2.6 %collective-permute-start.2 = (bf16[64,1024]{1,0:T(8,128)(2,1)S(1)}, bf16[64,1024]{1,0:T(8,128)(2,1)S(1)}, u32[]{:S(2)}, u32[]{:S(2)}) collective-permute-start(bf16[64,1024]{1,0:T(8,128)(2,1)S(1)} %inflow_join.1.refs_3_), channel_id=1, source_target_pairs={{0,6},{2,4},{4,2},{6,0},{8,14},{10,12},{12,10},{14,8},{1,7},{3,5},... | collective-permute-start | bytes 393224 | tf_op jit(solution)/shard_map/ppermute | solution.py:22
  11.4 0.5 %collective-permute-start.3 = (bf16[64,1024]{1,0:T(8,128)(2,1)S(1)}, bf16[64,1024]{1,0:T(8,128)(2,1)S(1)}, u32[]{:S(2)}, u32[]{:S(2)}) collective-permute-start(bf16[64,1024]{1,0:T(8,128)(2,1)S(1)} %inflow_join.1.refs_3_), channel_id=1, source_target_pairs={{0,2},{2,0},{4,6},{6,4},{8,10},{10,8},{12,14},{14,12},{1,3},{3,1},... | collective-permute-start | bytes 393224 | tf_op jit(solution)/shard_map/ppermute | solution.py:22
  11.9 0.4 %collective-permute-start.4 = (bf16[64,1024]{1,0:T(8,128)(2,1)S(1)}, bf16[64,1024]{1,0:T(8,128)(2,1)S(1)}, u32[]{:S(2)}, u32[]{:S(2)}) collective-permute-start(bf16[64,1024]{1,0:T(8,128)(2,1)S(1)} %inflow_join.1.refs_3_), channel_id=1, source_target_pairs={{0,4},{2,6},{4,0},{6,2},{8,12},{10,14},{12,8},{14,10},{1,5},{3,7},... | collective-permute-start | bytes 393224 | tf_op jit(solution)/shard_map/ppermute | solution.py:22
  13.0 3.0 %collective-permute-done.2.refs_4_ = bf16[64,1024]{1,0:T(8,128)(2,1)S(1)} collective-permute-done((bf16[64,1024]{1,0:T(8,128)(2,1)S(1)}, bf16[64,1024]{1,0:T(8,128)(2,1)S(1)}, u32[]{:S(2)}, u32[]{:S(2)}) %collective-permute-start.2) | collective-permute-done | bytes 131104 | tf_op jit(solution)/shard_map/ppermute | solution.py:22
  16.0 1.4 %collective-permute-done.3.refs_5_ = bf16[64,1024]{1,0:T(8,128)(2,1)S(1)} collective-permute-done((bf16[64,1024]{1,0:T(8,128)(2,1)S(1)}, bf16[64,1024]{1,0:T(8,128)(2,1)S(1)}, u32[]{:S(2)}, u32[]{:S(2)}) %collective-permute-start.3) | collective-permute-done | bytes 131104 | tf_op jit(solution)/shard_map/ppermute | solution.py:22
  17.4 0.1 collective-permute-done.4.refs_6_
  17.4 1.4 %cut_values.1 = (f32[2048,256]{1,0:T(8,128)S(1)}, f32[2,256]{1,0:T(2,128)S(1)}) custom-call(s32[1]{0:T(128)S(6)} %copy.9.refs_0_.counts_ref, bf16[2048,1024]{1,0:T(8,128)(2,1)S(1)} %get-tuple-element.13.refs_1_, f32[2048,128]{1,0:T(8,128)S(1)} %get-tuple-element.14.refs_2_, bf16[64,1024]{1,0:T(8,128)(2,1)S(1)} %inflow_join.1.refs_3_, ...), custom_call_target="tpu_custom_call" | custom-call | flops 1073741824 | bytes 4194304 | tf_op jit(solution)/shard_map/cut_values/pallas_call | solution.py:256
  18.8 0.1 collective-permute-start.5
  18.9 2.4 %collective-permute-start.6 = (f32[2,256]{1,0:T(2,128)S(1)}, f32[2,256]{1,0:T(2,128)S(1)}, u32[]{:S(2)}, u32[]{:S(2)}) collective-permute-start(f32[2,256]{1,0:T(2,128)S(1)} %get-tuple-element.20), channel_id=1, source_target_pairs={{0,9},{1,8},{2,11},{3,10},{4,13},{5,12},{6,15},{7,14},{8,1},{9,0},... | collective-permute-start | bytes 6152 | tf_op jit(solution)/shard_map/ppermute | solution.py:28
  21.3 1.0 %collective-permute-start.8 = (f32[2,256]{1,0:T(2,128)S(1)}, f32[2,256]{1,0:T(2,128)S(1)}, u32[]{:S(2)}, u32[]{:S(2)}) collective-permute-start(f32[2,256]{1,0:T(2,128)S(1)} %get-tuple-element.20), channel_id=1, source_target_pairs={{0,2},{2,0},{4,6},{6,4},{8,10},{10,8},{12,14},{14,12},{1,3},{3,1},... | collective-permute-start | bytes 6152 | tf_op jit(solution)/shard_map/ppermute | solution.py:22
  22.3 1.1 %collective-permute-start.9 = (f32[2,256]{1,0:T(2,128)S(1)}, f32[2,256]{1,0:T(2,128)S(1)}, u32[]{:S(2)}, u32[]{:S(2)}) collective-permute-start(f32[2,256]{1,0:T(2,128)S(1)} %get-tuple-element.20), channel_id=1, source_target_pairs={{0,10},{2,8},{4,14},{6,12},{8,2},{10,0},{12,6},{14,4},{1,11},{3,9}... | collective-permute-start | bytes 6152 | tf_op jit(solution)/shard_map/ppermute | solution.py:22
  23.4 0.0 collective-permute-done.5
  23.4 0.0 collective-permute-done.6
  23.5 1.3 %collective-permute-start.10 = (f32[2,256]{1,0:T(2,128)S(1)}, f32[2,256]{1,0:T(2,128)S(1)}, u32[]{:S(2)}, u32[]{:S(2)}) collective-permute-start(f32[2,256]{1,0:T(2,128)S(1)} %pad_maximum_fusion), channel_id=1, source_target_pairs={{0,7},{1,6},{2,5},{3,4},{4,3},{5,2},{6,1},{7,0},{8,15},{9,14},{10,... | collective-permute-start | bytes 6152 | tf_op jit(solution)/shard_map/ppermute | solution.py:28
  24.7 1.0 %collective-permute-start.11 = (f32[2,256]{1,0:T(2,128)S(1)}, f32[2,256]{1,0:T(2,128)S(1)}, u32[]{:S(2)}, u32[]{:S(2)}) collective-permute-start(f32[2,256]{1,0:T(2,128)S(1)} %pad_maximum_fusion), channel_id=1, source_target_pairs={{0,5},{1,4},{2,7},{3,6},{4,1},{5,0},{6,3},{7,2},{8,13},{9,12},{10,... | collective-permute-start | bytes 6152 | tf_op jit(solution)/shard_map/ppermute | solution.py:28
  25.7 0.0 collective-permute-start.7
  25.7 0.0 collective-permute-done.8.refs_1_
  25.7 2.0 %collective-permute-done.9.refs_2_ = f32[2,256]{1,0:T(2,128)S(1)} collective-permute-done((f32[2,256]{1,0:T(2,128)S(1)}, f32[2,256]{1,0:T(2,128)S(1)}, u32[]{:S(2)}, u32[]{:S(2)}) %collective-permute-start.9) | collective-permute-done | bytes 2080 | tf_op jit(solution)/shard_map/ppermute | solution.py:22
  27.7 0.0 collective-permute-done.10.refs_3_
  27.7 0.0 collective-permute-done.11.refs_4_
  27.7 0.0 collective-permute-done.7.refs_0_
  27.7 1.1 %margins.1 = bf16[2048,256]{1,0:T(8,128)(2,1)} custom-call(s32[1]{0:T(128)S(6)} %copy.9.refs_0_.counts_ref, f32[2048,256]{1,0:T(8,128)S(1)} %get-tuple-element.19.values_ref, f32[2,256]{1,0:T(2,128)S(1)} %collective-permute-done.7.refs_0_, f32[2,256]{1,0:T(2,128)S(1)} %collective-permute-done.8.refs_1_, f32[2,256]{1,0:T(2,128)S(1)} %collective-permute-done.9.refs_2_, ...), custom_call_target="tpu_custom_call" | custom-call | flops 2097152 | bytes 1048576 | tf_op jit(solution)/shard_map/margins/pallas_call | solution.py:281
  (2 shorter events, 0.0 us)
Async XLA Ops:
  0.0 7.9 %collective-permute-start = (bf16[32,1024]{1,0:T(8,128)(2,1)}, bf16[32,1024]{1,0:T(8,128)(2,1)S(1)}, u32[]{:S(2)}, u32[]{:S(2)}) collective-permute-start(bf16[32,1024]{1,0:T(8,128)(2,1)} %bitcast.3), channel_id=1, source_target_pairs={{0,8},{2,10},{4,12},{6,14},{8,0},{10,2},{12,4},{14,6},{1,9},{3,11}... | collective-permute-start | bytes 196616 | tf_op jit(solution)/shard_map/ppermute | solution.py:22
  4.0 4.6 %collective-permute-start.1 = (s32[1,32]{1,0:T(1,128)}, s32[1,32]{1,0:T(1,128)S(1)}, u32[]{:S(2)}, u32[]{:S(2)}) collective-permute-start(s32[1,32]{1,0:T(1,128)} %ids_hbm.1), channel_id=1, source_target_pairs={{0,8},{2,10},{4,12},{6,14},{8,0},{10,2},{12,4},{14,6},{1,9},{3,11}... | collective-permute-start | bytes 392 | tf_op jit(solution)/shard_map/ppermute | solution.py:22
  8.8 7.2 %collective-permute-start.2 = (bf16[64,1024]{1,0:T(8,128)(2,1)S(1)}, bf16[64,1024]{1,0:T(8,128)(2,1)S(1)}, u32[]{:S(2)}, u32[]{:S(2)}) collective-permute-start(bf16[64,1024]{1,0:T(8,128)(2,1)S(1)} %inflow_join.1.refs_3_), channel_id=1, source_target_pairs={{0,6},{2,4},{4,2},{6,0},{8,14},{10,12},{12,10},{14,8},{1,7},{3,5},... | collective-permute-start | bytes 393224 | tf_op jit(solution)/shard_map/ppermute | solution.py:22
  11.4 6.0 %collective-permute-start.3 = (bf16[64,1024]{1,0:T(8,128)(2,1)S(1)}, bf16[64,1024]{1,0:T(8,128)(2,1)S(1)}, u32[]{:S(2)}, u32[]{:S(2)}) collective-permute-start(bf16[64,1024]{1,0:T(8,128)(2,1)S(1)} %inflow_join.1.refs_3_), channel_id=1, source_target_pairs={{0,2},{2,0},{4,6},{6,4},{8,10},{10,8},{12,14},{14,12},{1,3},{3,1},... | collective-permute-start | bytes 393224 | tf_op jit(solution)/shard_map/ppermute | solution.py:22
  11.9 5.5 %collective-permute-start.4 = (bf16[64,1024]{1,0:T(8,128)(2,1)S(1)}, bf16[64,1024]{1,0:T(8,128)(2,1)S(1)}, u32[]{:S(2)}, u32[]{:S(2)}) collective-permute-start(bf16[64,1024]{1,0:T(8,128)(2,1)S(1)} %inflow_join.1.refs_3_), channel_id=1, source_target_pairs={{0,4},{2,6},{4,0},{6,2},{8,12},{10,14},{12,8},{14,10},{1,5},{3,7},... | collective-permute-start | bytes 393224 | tf_op jit(solution)/shard_map/ppermute | solution.py:22
  18.8 4.6 %collective-permute-start.5 = (f32[2,256]{1,0:T(2,128)S(1)}, f32[2,256]{1,0:T(2,128)S(1)}, u32[]{:S(2)}, u32[]{:S(2)}) collective-permute-start(f32[2,256]{1,0:T(2,128)S(1)} %get-tuple-element.20), channel_id=1, source_target_pairs={{0,1},{1,0},{2,3},{3,2},{4,5},{5,4},{6,7},{7,6},{8,9},{9,8},{10,11... | collective-permute-start | bytes 6152 | tf_op jit(solution)/shard_map/ppermute | solution.py:28
  18.9 4.5 %collective-permute-start.6 = (f32[2,256]{1,0:T(2,128)S(1)}, f32[2,256]{1,0:T(2,128)S(1)}, u32[]{:S(2)}, u32[]{:S(2)}) collective-permute-start(f32[2,256]{1,0:T(2,128)S(1)} %get-tuple-element.20), channel_id=1, source_target_pairs={{0,9},{1,8},{2,11},{3,10},{4,13},{5,12},{6,15},{7,14},{8,1},{9,0},... | collective-permute-start | bytes 6152 | tf_op jit(solution)/shard_map/ppermute | solution.py:28
  21.3 4.4 %collective-permute-start.8 = (f32[2,256]{1,0:T(2,128)S(1)}, f32[2,256]{1,0:T(2,128)S(1)}, u32[]{:S(2)}, u32[]{:S(2)}) collective-permute-start(f32[2,256]{1,0:T(2,128)S(1)} %get-tuple-element.20), channel_id=1, source_target_pairs={{0,2},{2,0},{4,6},{6,4},{8,10},{10,8},{12,14},{14,12},{1,3},{3,1},... | collective-permute-start | bytes 6152 | tf_op jit(solution)/shard_map/ppermute | solution.py:22
  22.3 5.4 %collective-permute-start.9 = (f32[2,256]{1,0:T(2,128)S(1)}, f32[2,256]{1,0:T(2,128)S(1)}, u32[]{:S(2)}, u32[]{:S(2)}) collective-permute-start(f32[2,256]{1,0:T(2,128)S(1)} %get-tuple-element.20), channel_id=1, source_target_pairs={{0,10},{2,8},{4,14},{6,12},{8,2},{10,0},{12,6},{14,4},{1,11},{3,9}... | collective-permute-start | bytes 6152 | tf_op jit(solution)/shard_map/ppermute | solution.py:22
  23.5 4.3 %collective-permute-start.10 = (f32[2,256]{1,0:T(2,128)S(1)}, f32[2,256]{1,0:T(2,128)S(1)}, u32[]{:S(2)}, u32[]{:S(2)}) collective-permute-start(f32[2,256]{1,0:T(2,128)S(1)} %pad_maximum_fusion), channel_id=1, source_target_pairs={{0,7},{1,6},{2,5},{3,4},{4,3},{5,2},{6,1},{7,0},{8,15},{9,14},{10,... | collective-permute-start | bytes 6152 | tf_op jit(solution)/shard_map/ppermute | solution.py:28
  24.7 3.0 %collective-permute-start.11 = (f32[2,256]{1,0:T(2,128)S(1)}, f32[2,256]{1,0:T(2,128)S(1)}, u32[]{:S(2)}, u32[]{:S(2)}) collective-permute-start(f32[2,256]{1,0:T(2,128)S(1)} %pad_maximum_fusion), channel_id=1, source_target_pairs={{0,5},{1,4},{2,7},{3,6},{4,1},{5,0},{6,3},{7,2},{8,13},{9,12},{10,... | collective-permute-start | bytes 6152 | tf_op jit(solution)/shard_map/ppermute | solution.py:28
  25.7 2.0 %collective-permute-start.7 = (f32[2,256]{1,0:T(2,128)S(1)}, f32[2,256]{1,0:T(2,128)S(1)}, u32[]{:S(2)}, u32[]{:S(2)}) collective-permute-start(f32[2,256]{1,0:T(2,128)S(1)} %pad_maximum_fusion), channel_id=1, source_target_pairs={{0,1},{1,0},{2,3},{3,2},{4,5},{5,4},{6,7},{7,6},{8,9},{9,8},{10,11... | collective-permute-start | bytes 6152 | tf_op jit(solution)/shard_map/ppermute | solution.py:28
